TPU v7x, 256 devices: a whole 4x4x8 slice. The times are simulated.
256 devices in a mesh: seq: 32 (over x, z), tp: 8 (over y, core).
Axes of the slice: x: 4, y: 4, z: 8, core: 2. Of those that a mesh axis runs over, the one named last changes fastest.
Arguments:
- global_out: bfloat16 [4096, 8192], P('seq', 'tp'), may hold values from -6 to 6
- in_nibbles: int32 [2, 4096, 8], P(None, ('seq', 'tp')), may hold values from 0 to 15
- target_nibbles: int32 [2, 4096, 8], P(None, ('seq', 'tp')), may hold values from 0 to 15
- proj_weight: bfloat16 [1024, 768], replicated, may hold values from -0.1875 to 0.1875
- attn_weight: bfloat16 [4, 768, 768], replicated, may hold values from -0.21875 to 0.21875
- head_weight: bfloat16 [768, 32], replicated, may hold values from -0.625 to 0.625
- byte_embed: bfloat16 [32, 768], replicated, may hold values from -6 to 6
- lo_table: float32 [16, 16], replicated, may hold values from -6 to 6
Outputs:
- grad_global: bfloat16 [4096, 8192], P('seq', 'tp')
- grad_proj: float32 [1024, 768], P(('seq', 'tp'))
- grad_attn: float32 [589824], P(('seq', 'tp'))
- grad_head: float32 [768, 32], replicated
- grad_embed: float32 [32, 768], replicated
- grad_table: float32 [16, 16], replicated
- mean_loss: float32 [], replicated
All inputs are finite; a program needn't handle non-finite values.
Results may differ from a plain program's by a relative error of at most 0.012.
Values may be sent and summed in bfloat16 or wider, within the bound.
No kernel may reach another device: no remote copies, remote signals or barrier semaphores. Data moves between devices by JAX's collectives and lax.ppermute only.
A program may use at most 64 MiB of HBM per device.

v0:
```python
import jax
import jax.numpy as jnp
from jax import lax
from jax.sharding import PartitionSpec as P

HEADS = 12
HS = 64
K = 8


norm_eps = 1e-06


def to_low(tensor):
    return lax.optimization_barrier(tensor.astype(jnp.bfloat16))


def inverse_rms(values):
    return lax.rsqrt(jnp.mean(values * values, axis=-1, keepdims=True) + norm_eps)


def norm_backward(values, inverse, upstream):
    summed = jnp.sum(upstream * values, axis=-1, keepdims=True) / values.shape[-1]
    return inverse * (upstream - values * (inverse * inverse) * summed)


def contract_rows(left_side, right_side, precision=None):
    return lax.dot_general(
        left_side,
        right_side,
        (((0,), (0,)), ((), ())),
        preferred_element_type=jnp.float32,
        precision=precision,
    )


def contract_cols(left_side, right_side):
    return lax.dot_general(
        left_side, right_side, (((1,), (1,)), ((), ())), preferred_element_type=jnp.float32
    )


def softmax_rows(logits):
    shifted = logits - jnp.max(logits, axis=-1, keepdims=True)
    exponent = jnp.exp(shifted)
    return exponent / jnp.sum(exponent, axis=-1, keepdims=True)


def row_loss(row_logits, onehot):
    row_max = jnp.max(row_logits, axis=-1)
    total = jnp.sum(jnp.exp(row_logits - row_max[:, None]), axis=-1)
    return row_max + jnp.log(total) - jnp.sum(row_logits * onehot, axis=-1)


def local_pass(projected, in_nib, tgt_nib, attn_weight, head_weight, byte_embed, lo_table):
    row_count, feat_width = projected.shape
    nibble = lo_table.shape[0]
    patch_count = row_count // K
    code_list = jnp.arange(2 * nibble, dtype=jnp.int32)
    in_onehot = jnp.logical_or(
        in_nib[0][:, None] == code_list[None, :], in_nib[1][:, None] + nibble == code_list[None, :]
    ).astype(jnp.bfloat16)
    state_in = projected.astype(jnp.float32) + jnp.dot(
        in_onehot, byte_embed, preferred_element_type=jnp.float32
    )
    inv_in = inverse_rms(state_in)
    normed_in = to_low(state_in * inv_in)
    query = to_low(jnp.dot(normed_in, attn_weight[0], preferred_element_type=jnp.float32))
    keys_all = to_low(jnp.dot(normed_in, attn_weight[1], preferred_element_type=jnp.float32))
    values_all = to_low(jnp.dot(normed_in, attn_weight[2], preferred_element_type=jnp.float32))

    def split_heads(tensor):
        return tensor.reshape(patch_count, K, HEADS, HS).astype(jnp.float32)

    query_h = split_heads(query)
    keys_h = split_heads(keys_all)
    values_h = split_heads(values_all)
    score_scale = 1.0 / HS**0.5
    scores = jnp.einsum("pqhd,pkhd->phqk", query_h, keys_h) * score_scale
    causal = lax.broadcasted_iota(jnp.int32, (K, K), 0) >= lax.broadcasted_iota(
        jnp.int32, (K, K), 1
    )
    scores = jnp.where(causal, scores, -1e30)
    attn_probs = softmax_rows(scores)
    probs_low = to_low(attn_probs).astype(jnp.float32)
    context = to_low(
        jnp.einsum("phqk,pkhd->pqhd", probs_low, values_h).reshape(row_count, feat_width)
    )
    state_mid = state_in + jnp.dot(context, attn_weight[3], preferred_element_type=jnp.float32)
    inv_mid = inverse_rms(state_mid)
    normed_mid = to_low(state_mid * inv_mid)
    logits = jnp.dot(normed_mid, head_weight, preferred_element_type=jnp.float32)
    nib_codes = jnp.arange(nibble, dtype=jnp.int32)
    hi_onehot = (tgt_nib[0][:, None] == nib_codes[None, :]).astype(jnp.float32)
    lo_onehot = (tgt_nib[1][:, None] == nib_codes[None, :]).astype(jnp.float32)
    hi_logits = logits[:, :nibble]
    lo_logits = logits[:, nibble:] + jnp.dot(
        hi_onehot, lo_table, precision=lax.Precision.HIGHEST, preferred_element_type=jnp.float32
    )
    loss_sum = jnp.sum(row_loss(hi_logits, hi_onehot) + row_loss(lo_logits, lo_onehot))
    grad_hi = softmax_rows(hi_logits) - hi_onehot
    grad_lo = softmax_rows(lo_logits) - lo_onehot
    grad_table = contract_rows(hi_onehot, grad_lo, lax.Precision.HIGHEST)
    grad_logits = to_low(jnp.concatenate([grad_hi, grad_lo], axis=1))
    grad_head = contract_rows(normed_mid, grad_logits)
    grad_mid = norm_backward(state_mid, inv_mid, contract_cols(grad_logits, head_weight))
    grad_mid_low = to_low(grad_mid)
    grad_context = to_low(contract_cols(grad_mid_low, attn_weight[3]))
    grad_ctx_h = split_heads(grad_context)
    grad_probs = jnp.einsum("pqhd,pkhd->phqk", grad_ctx_h, values_h)
    grad_values = to_low(
        jnp.einsum("phqk,pqhd->pkhd", probs_low, grad_ctx_h).reshape(row_count, feat_width)
    )
    grad_scores = to_low(
        attn_probs
        * (grad_probs - jnp.sum(grad_probs * attn_probs, axis=-1, keepdims=True))
        * score_scale
    )
    grad_scores_f = grad_scores.astype(jnp.float32)
    grad_query = to_low(
        jnp.einsum("phqk,pkhd->pqhd", grad_scores_f, keys_h).reshape(row_count, feat_width)
    )
    grad_keys = to_low(
        jnp.einsum("phqk,pqhd->pkhd", grad_scores_f, query_h).reshape(row_count, feat_width)
    )
    grad_value_weight = contract_rows(normed_in, grad_values)
    grad_normed_in = (
        contract_cols(grad_query, attn_weight[0])
        + contract_cols(grad_keys, attn_weight[1])
        + contract_cols(grad_values, attn_weight[2])
    )
    grad_in = grad_mid + norm_backward(state_in, inv_in, grad_normed_in)
    grad_embed = contract_rows(in_onehot.astype(jnp.float32), grad_in, lax.Precision.HIGHEST)
    return (loss_sum, to_low(grad_in), grad_value_weight, grad_head, grad_embed, grad_table)


def local(
    global_out,
    in_nibbles,
    target_nibbles,
    proj_weight,
    attn_weight,
    head_weight,
    byte_embed,
    lo_table,
):
    tp_count = lax.axis_size("tp")
    seq_rows = global_out.shape[0]
    owned_patches = seq_rows // tp_count
    pos_width = proj_weight.shape[0]
    feat_width = proj_weight.shape[1]
    total_rows = owned_patches * K
    in_flat = in_nibbles.reshape(2, total_rows)
    tgt_flat = target_nibbles.reshape(2, total_rows)
    full_rows = lax.all_to_all(global_out, "tp", split_axis=0, concat_axis=1, tiled=True)
    pos_rows = full_rows.reshape(total_rows, pos_width)
    projected = to_low(jnp.dot(pos_rows, proj_weight, preferred_element_type=jnp.float32))
    loss_sum, grad_rows, part_value, part_head, part_embed, part_table = local_pass(
        projected, in_flat, tgt_flat, attn_weight, head_weight, byte_embed, lo_table
    )
    grad_pos = to_low(contract_cols(grad_rows, proj_weight)).reshape(owned_patches, K * pos_width)
    grad_global = lax.all_to_all(grad_pos, "tp", split_axis=1, concat_axis=0, tiled=True)
    part_proj = contract_rows(pos_rows, grad_rows)
    value_flat = part_value.reshape(feat_width * feat_width)
    grad_proj, grad_attn = (
        lax.psum_scatter(part_proj, ("seq", "tp"), scatter_dimension=0, tiled=True),
        lax.psum_scatter(value_flat, ("seq", "tp"), scatter_dimension=0, tiled=True),
    )
    loss_total, grad_head, grad_embed, grad_table = lax.psum(
        (loss_sum, part_head, part_embed, part_table), ("seq", "tp")
    )
    mean_loss = loss_total / (total_rows * lax.axis_size("seq") * tp_count)
    return (grad_global, grad_proj, grad_attn, grad_head, grad_embed, grad_table, mean_loss)


def solution(mesh):
    in_specs = (
        P("seq", "tp"),
        P(None, ("seq", "tp"), None),
        P(None, ("seq", "tp"), None),
        P(),
        P(),
        P(),
        P(),
        P(),
    )
    out_specs = (P("seq", "tp"), P(("seq", "tp"), None), P(("seq", "tp")), P(), P(), P(), P())
    return jax.shard_map(local, mesh=mesh, in_specs=in_specs, out_specs=out_specs, check_vma=False)
```

profile of v0, /device:TPU:32, one launch (start us, length us, event | category | flops | bytes accessed | tf_op | source)
XLA Modules:
  0.0 364.6 jit_solution(16135195104714063232)
XLA Ops:
  7.2 4.6 %all-to-all-start = ((bf16[8,16,1024]{2,1,0:T(8,128)(2,1)}), bf16[8,16,1024]{2,1,0:T(8,128)(2,1)S(1)}, u32[]{:S(2)}, u32[]{:S(2)}) async-start(bf16[8,16,1024]{2,1,0:T(8,128)(2,1)} %bitcast.86), calls=%async_computation | async-start | bytes 524288 | tf_op jit(solution)/shard_map/all_to_all | solution.py:155
  11.8 0.7 fusion.84
  12.9 0.7 fusion.83
  14.5 4.9 %all-to-all-done = bf16[8,16,1024]{2,1,0:T(8,128)(2,1)S(1)} async-done(((bf16[8,16,1024]{2,1,0:T(8,128)(2,1)}), bf16[8,16,1024]{2,1,0:T(8,128)(2,1)S(1)}, u32[]{:S(2)}, u32[]{:S(2)}) %all-to-all-start) | async-done | bytes 262176 | tf_op jit(solution)/shard_map/all_to_all | solution.py:155
  20.8 1.7 fusion.29
  22.9 1.0 fusion.26
  24.6 1.6 fusion.85
  26.2 0.6 copy-done.12
  26.8 1.2 fusion.81
  28.0 1.3 reshape.111
  29.8 0.9 copy.79
  30.7 2.1 convert_element_type.99
  32.7 1.8 multiply_reduce_fusion.3
  34.7 1.0 fusion.91
  35.8 0.9 fusion.90
  37.2 1.2 select_reduce_fusion
  38.4 0.7 subtract_convert_fusion
  39.1 1.1 multiply_reduce_fusion.2
  40.9 2.5 fusion.35
  43.4 2.1 reshape.114
  45.5 1.5 fusion.12
  47.0 1.5 fusion.48
  49.6 1.1 fusion.11
  50.7 1.2 fusion.10
  51.9 0.8 fusion.93
  52.7 0.9 copy.90
  53.6 1.4 convert_element_type.114
  55.0 1.9 fusion.92
  56.9 3.2 reshape.115
  60.1 1.9 copy.88
  62.0 1.4 convert_element_type.111
  63.4 1.9 copy.86
  65.3 2.1 convert_element_type.108
  67.4 1.9 fusion.19
  69.4 1.8 convolution_add_fusion.1
  71.2 1.9 multiply_reduce_fusion.1
  73.4 2.3 convolution_bitcast_fusion
  75.7 1.0 fusion.61
  77.4 0.9 copy.91
  78.3 3.4 all-to-all-start.1
  82.5 81.2 %all-reduce.2 = (f32[16,16]{1,0:T(8,128)}, f32[]{:T(128)}) all-reduce(f32[16,16]{1,0:T(8,128)S(1)} %fusion.68, f32[]{:T(128)} %add_reduce_fusion), channel_id=1, replica_groups=mesh['seq'=32,'tp'=8] {'seq','tp'}, use_global_device_ids=true, to_apply=%region_15.16 | all-reduce | flops 257 | bytes 2056 | tf_op jit(solution)/shard_map/psum | solution.py:169
  164.4 185.1 %all-reduce.6.cloned.1.call-done = (f32[1024,768]{0,1:T(8,128)}, f32[589824]{0:T(1024)}, f32[768,32]{0,1:T(8,128)}, f32[32,768]{1,0:T(8,128)}) async-done(((f32[1024,768]{0,1:T(8,128)}, f32[589824]{0:T(1024)}, f32[768,32]{0,1:T(8,128)}, f32[32,768]{1,0:T(8,128)}), (f32[1024,768]{0,1:T(8,128)}, f32[589824]{0:T(1024)}, f32[768,32]{0,1:T(8,128)}, f32[32,768]{1,0:T(8,128)})) %all-reduce.6.cloned.1.call-update) | async-done | bytes 5701648
  349.5 1.2 constant_dynamic-slice_fusion
  350.7 0.8 copy.92
  351.4 1.4 dynamic-slice.1
  352.8 0.7 copy.134
  353.5 1.5 copy.135
  355.1 1.5 copy.136
  (114 shorter events, 8.1 us)
Async XLA Ops:
  7.2 12.2 %copy-start = (bf16[1024,768]{1,0:T(8,128)(2,1)S(1)}, bf16[1024,768]{1,0:T(8,128)(2,1)}, u32[]{:S(2)}) copy-start(bf16[1024,768]{1,0:T(8,128)(2,1)} %param.11) | copy-start | bytes 4718596
  7.2 12.6 %copy-start.14 = (bf16[32,768]{1,0:T(8,128)(2,1)S(1)}, bf16[32,768]{1,0:T(8,128)(2,1)}, u32[]{:S(2)}) copy-start(bf16[32,768]{1,0:T(8,128)(2,1)} %param.14) | copy-start | bytes 147460
  7.2 12.2 %all-to-all-start = ((bf16[8,16,1024]{2,1,0:T(8,128)(2,1)}), bf16[8,16,1024]{2,1,0:T(8,128)(2,1)S(1)}, u32[]{:S(2)}, u32[]{:S(2)}) async-start(bf16[8,16,1024]{2,1,0:T(8,128)(2,1)} %bitcast.86), calls=%async_computation | async-start | bytes 524288 | tf_op jit(solution)/shard_map/all_to_all | solution.py:155
  11.8 337.7 %all-reduce.6.cloned.1.call-start = ((), (), s32[]{:S(2)}) async-start(), calls=%async_computation.2 | async-start | bytes 11403264
  12.7 9.8 %copy-start.28 = (s32[128]{0:T(128)}, s32[128]{0:T(128)S(1)}, u32[]{:S(2)}) copy-start(s32[128]{0:T(128)S(1)} %add.77) | copy-start | bytes 1540
  12.9 9.6 %copy-start.30 = (s32[128]{0:T(128)}, s32[128]{0:T(128)S(1)}, u32[]{:S(2)}) copy-start(s32[128]{0:T(128)S(1)} %eq.58) | copy-start | bytes 1540
  13.8 24.6 %copy-start.17 = (s32[128]{0:T(128)}, s32[128]{0:T(128)S(1)}, u32[]{:S(2)}) copy-start(s32[128]{0:T(128)S(1)} %eq.65) | copy-start | bytes 1540
  19.3 3.1 copy-start.1
  20.7 2.1 copy-start.38
  20.8 2.1 copy-start.10
  24.2 2.0 copy-start.5
  24.5 1.6 copy-start.7
  26.2 0.6 copy-start.12
  29.3 5.2 %copy-start.2 = (bf16[16,8,12,64]{3,2,1,0:T(8,128)(2,1)}, bf16[16,8,12,64]{3,2,1,0:T(8,128)(2,1)S(1)}, u32[]{:S(2)}) copy-start(bf16[16,8,12,64]{3,2,1,0:T(8,128)(2,1)S(1)} %reshape.111) | copy-start | bytes 589828
  34.6 5.7 %copy-start.26 = (f32[128]{0:T(128)}, f32[128]{0:T(128)S(1)}, u32[]{:S(2)}) copy-start(f32[128]{0:T(128)S(1)} %get-tuple-element.54) | copy-start | bytes 1540
  34.6 5.7 %copy-start.32 = (f32[128]{0:T(128)}, f32[128]{0:T(128)S(1)}, u32[]{:S(2)}) copy-start(f32[128]{0:T(128)S(1)} %get-tuple-element.53) | copy-start | bytes 1540
  34.7 4.4 %copy-start.3 = (bf16[128,768]{1,0:T(8,128)(2,1)}, bf16[128,768]{1,0:T(8,128)(2,1)S(1)}, u32[]{:S(2)}) copy-start(bf16[128,768]{1,0:T(8,128)(2,1)S(1)} %multiply_convert_fusion) | copy-start | bytes 589828
  35.7 3.3 copy-start.15
  36.7 2.4 copy-start.20
  37.2 1.9 copy-start.24
  38.4 0.7 copy-start.22
  40.3 0.5 copy-start.34
  40.9 7.6 %copy-start.13 = (f32[16,12,8]{2,1,0:T(8,128)S(1)}, f32[16,12,8]{2,1,0:T(8,128)}, u32[]{:S(2)}) copy-start(f32[16,12,8]{2,1,0:T(8,128)} %copy-done.12) | copy-start | bytes 18436
  45.5 3.0 copy-start.9
  48.5 1.0 copy-start.6
  48.6 2.2 copy-start.8
  49.6 2.3 copy-start.4
  49.6 5.4 %copy-start.11 = (bf16[128,768]{1,0:T(8,128)(2,1)S(1)}, bf16[128,768]{1,0:T(8,128)(2,1)}, u32[]{:S(2)}) copy-start(bf16[128,768]{1,0:T(8,128)(2,1)} %copy-done.10) | copy-start | bytes 589828
  69.3 3.8 %copy-start.27 = (f32[128]{0:T(128)S(1)}, f32[128]{0:T(128)}, u32[]{:S(2)}) copy-start(f32[128]{0:T(128)} %copy-done.26) | copy-start | bytes 1540
  69.3 3.8 %copy-start.33 = (f32[128]{0:T(128)S(1)}, f32[128]{0:T(128)}, u32[]{:S(2)}) copy-start(f32[128]{0:T(128)} %copy-done.32) | copy-start | bytes 1540
  69.3 3.8 %copy-start.35 = (f32[128]{0:T(128)S(1)}, f32[128]{0:T(128)}, u32[]{:S(2)}) copy-start(f32[128]{0:T(128)} %copy-done.34) | copy-start | bytes 1540
  69.3 3.8 %copy-start.39 = (f32[128]{0:T(128)S(1)}, f32[128]{0:T(128)}, u32[]{:S(2)}) copy-start(f32[128]{0:T(128)} %copy-done.38) | copy-start | bytes 1540
  69.4 3.8 %copy-start.40 = (f32[128]{0:T(128)S(1)}, f32[128]{0:T(128)}, u32[]{:S(2)}) copy-start(f32[128]{0:T(128)} %get-tuple-element.51) | copy-start | bytes 1540
  73.2 2.5 copy-start.29
  73.2 2.5 copy-start.31
  76.7 5.0 %copy-start.16 = (f32[128]{0:T(128)S(1)}, f32[128]{0:T(128)}, u32[]{:S(2)}) copy-start(f32[128]{0:T(128)} %copy-done.15) | copy-start | bytes 1540
  76.7 5.0 %copy-start.21 = (f32[128]{0:T(128)S(1)}, f32[128]{0:T(128)}, u32[]{:S(2)}) copy-start(f32[128]{0:T(128)} %copy-done.20) | copy-start | bytes 1540
  76.7 5.0 %copy-start.23 = (f32[128]{0:T(128)S(1)}, f32[128]{0:T(128)}, u32[]{:S(2)}) copy-start(f32[128]{0:T(128)} %copy-done.22) | copy-start | bytes 1540
  76.7 5.0 %copy-start.25 = (f32[128]{0:T(128)S(1)}, f32[128]{0:T(128)}, u32[]{:S(2)}) copy-start(f32[128]{0:T(128)} %copy-done.24) | copy-start | bytes 1540
  76.7 5.0 %copy-start.36 = (f32[128]{0:T(128)S(1)}, f32[128]{0:T(128)}, u32[]{:S(2)}) copy-start(f32[128]{0:T(128)} %get-tuple-element.35) | copy-start | bytes 1540
  76.7 5.0 %copy-start.37 = (f32[128]{0:T(128)S(1)}, f32[128]{0:T(128)}, u32[]{:S(2)}) copy-start(f32[128]{0:T(128)} %get-tuple-element.37) | copy-start | bytes 1540
  76.7 5.6 %copy-start.18 = (s32[128]{0:T(128)S(1)}, s32[128]{0:T(128)}, u32[]{:S(2)}) copy-start(s32[128]{0:T(128)} %copy-done.17) | copy-start | bytes 1540
  76.8 5.6 %copy-start.19 = (s32[128]{0:T(128)S(1)}, s32[128]{0:T(128)}, u32[]{:S(2)}) copy-start(s32[128]{0:T(128)} %eq.69) | copy-start | bytes 1540
  78.3 86.1 %all-to-all-start.1 = ((bf16[16,8,1024]{2,0,1:T(8,128)(2,1)}), bf16[16,8,1024]{2,0,1:T(8,128)(2,1)S(1)}, u32[]{:S(2)}, u32[]{:S(2)}) async-start(bf16[16,8,1024]{2,0,1:T(8,128)(2,1)} %copy.91), calls=%async_computation.1 | async-start | bytes 524288 | tf_op jit(solution)/shard_map/all_to_all | solution.py:162
Sparse Core Ops, SparseCore 0:
  76.8 272.6 all-reduce.5
where the time goes:
time: 369 us; the launch traced here: 365 us
  waiting for transfers between devices  190 us (51%)
  blocking collectives  81.2 us (22%)
  local copies, waits for them, and re-layouts  31.4 us (9%)
  matrix products  30.8 us (8%)
  between operations  16.5 us (4%)
  starting transfers between devices  8.06 us (2%)
  other arithmetic  6.51 us (2%)
    unnamed x2, waiting for transfers between devices  185 us
    psum x1, blocking collectives, local(): lax.psum((loss_sum, part_head, part_embed, part_table), ('seq', 'tp'))  81.2 us
    convert_element_type x8, local copies, waits for them, and re-layouts, to_low(): return lax.optimization_barrier(tensor.astype(jnp.bfloat16))  12.5 us
    dot_general x6, matrix products, contract_cols(): lax.dot_general(left_side, right_side, (((1,), (1,)), ((), ())), preferre...  9.92 us
    unnamed x88, local copies, waits for them, and re-layouts  8.99 us
  transfers between devices with their start and end apart: 3, of which 2 were waited for; matrix products, arithmetic and copies ran while one was open for 1% of the time, Pallas kernels for 0%

commit v1 on v0

v1 whole, which is shorter than its diff:
```python
import jax
import jax.numpy as jnp
from jax import lax
from jax.experimental import pallas as pl
from jax.experimental.pallas import tpu as pltpu
from jax.sharding import Mesh, PartitionSpec as P

HEADS = 12
HS = 64
K = 8
PD = 16
ROWS = K * PD
D = 768
DGT = 1024
NIB = 16
LANES = 128
TILES = D // LANES
EPS = 1e-06
F32 = jnp.float32
BF16 = jnp.bfloat16
NX, NZ, NY, NC = 4, 8, 4, 2
BLK = 64
TOTAL_BYTES = 32768


def mm(a, b):
    return jnp.dot(a, b, preferred_element_type=F32)


def mm_t(a, b):
    return lax.dot_general(a, b, (((1,), (1,)), ((), ())), preferred_element_type=F32)


def tmm(a, b, precision=None):
    return lax.dot_general(
        a, b, (((0,), (0,)), ((), ())), preferred_element_type=F32, precision=precision
    )


def norm_backward(values, inverse, upstream):
    summed = jnp.sum(upstream * values, axis=-1, keepdims=True) / D
    return inverse * (upstream - values * (inverse * inverse) * summed)


def owner_columns(size, piece, core):
    block = NZ * NY * NC * piece
    src = lax.broadcasted_iota(jnp.int32, (size, size), 0)
    dst = lax.broadcasted_iota(jnp.int32, (size, size), 1)
    xb = dst // block
    w = dst - xb * block
    half = w // (block // 2)
    w = w - half * (block // 2)
    y = w // (NZ * piece)
    w = w - y * (NZ * piece)
    z = w // piece
    i = w - z * piece
    c = jnp.where(half == 0, 1 - core, core)
    want = xb * block + z * (NY * NC * piece) + y * (NC * piece) + c * piece + i
    return (src == want).astype(BF16)


def softmax_cols(logits):
    e = jnp.exp(logits - jnp.max(logits, axis=0, keepdims=True))
    return e / jnp.sum(e, axis=0, keepdims=True)


def col_loss(logits, onehot):
    top = jnp.max(logits, axis=0, keepdims=True)
    total = jnp.sum(jnp.exp(logits - top), axis=0, keepdims=True)
    return top + jnp.log(total) - jnp.sum(logits * onehot, axis=0, keepdims=True)


def main_kernel(
    pos_ref, nib_ref, proj_ref, attn_ref, head_ref, embed_ref, lo_ref, send_ref, keep_ref, rows_ref
):
    core = lax.axis_index("c")
    pos = pos_ref[...]
    projected = mm(pos, proj_ref[...]).astype(BF16).astype(F32)
    codes = lax.broadcasted_iota(jnp.int32, (2 * NIB, ROWS), 0)
    in_hot = jnp.logical_or(codes == nib_ref[0:1, :], codes == nib_ref[1:2, :] + NIB).astype(BF16)
    state_in = projected + tmm(in_hot, embed_ref[...])
    inv_in = lax.rsqrt(jnp.mean(state_in * state_in, axis=-1, keepdims=True) + EPS)
    normed_in = (state_in * inv_in).astype(BF16)
    query = mm(normed_in, attn_ref[0]).astype(BF16)
    keys = mm(normed_in, attn_ref[1]).astype(BF16)
    values = mm(normed_in, attn_ref[2]).astype(BF16)

    key_row = lax.broadcasted_iota(jnp.int32, (ROWS, 2 * ROWS), 0)
    query_row = lax.broadcasted_iota(jnp.int32, (ROWS, 2 * ROWS), 1) % ROWS
    allowed = jnp.logical_and(key_row % PD == query_row % PD, key_row <= query_row)
    lane = lax.broadcasted_iota(jnp.int32, (2 * ROWS, LANES), 1)
    part = lax.broadcasted_iota(jnp.int32, (2 * ROWS, LANES), 0)
    own = ((lane // HS) == (part // ROWS)).astype(BF16)

    def two_heads(tile):
        return jnp.concatenate([tile, tile], axis=0) * own

    def stacked(cols):
        return jnp.concatenate([cols[:, :ROWS], cols[:, ROWS:]], axis=0)

    scale = 1.0 / HS**0.5
    probs, probs_low, contexts = [], [], []
    for t in range(TILES):
        cut = slice(t * LANES, (t + 1) * LANES)
        scores = mm_t(keys[:, cut], two_heads(query[:, cut])) * scale
        p = softmax_cols(jnp.where(allowed, scores, -1e30))
        low = p.astype(BF16)
        probs.append(p)
        probs_low.append(low)
        contexts.append(tmm(stacked(low), two_heads(values[:, cut])).astype(BF16))
    context = jnp.concatenate(contexts, axis=1)
    state_mid = state_in + mm(context, attn_ref[3])
    inv_mid = lax.rsqrt(jnp.mean(state_mid * state_mid, axis=-1, keepdims=True) + EPS)
    normed_mid = (state_mid * inv_mid).astype(BF16)

    logits = mm_t(head_ref[...], normed_mid)
    nib_codes = lax.broadcasted_iota(jnp.int32, (NIB, ROWS), 0)
    hi_hot = (nib_codes == nib_ref[2:3, :]).astype(F32)
    lo_hot = (nib_codes == nib_ref[3:4, :]).astype(F32)
    hi_logits = logits[:NIB]
    lo_logits = logits[NIB:] + jnp.dot(
        lo_ref[...], hi_hot, precision=lax.Precision.HIGHEST, preferred_element_type=F32
    )
    loss = col_loss(hi_logits, hi_hot) + col_loss(lo_logits, lo_hot)
    grad_hi = softmax_cols(hi_logits) - hi_hot
    grad_lo = softmax_cols(lo_logits) - lo_hot
    grad_table = lax.dot_general(
        hi_hot,
        jnp.concatenate([grad_lo, jnp.zeros((LANES - NIB, ROWS), F32)], axis=0),
        (((1,), (1,)), ((), ())),
        preferred_element_type=F32,
        precision=lax.Precision.HIGHEST,
    )
    grad_logits = jnp.concatenate([grad_hi, grad_lo], axis=0).astype(BF16)
    grad_head = mm(grad_logits, normed_mid)
    grad_mid = norm_backward(state_mid, inv_mid, tmm(grad_logits, head_ref[...]))
    grad_context = mm_t(grad_mid.astype(BF16), attn_ref[3]).astype(BF16)

    grad_q, grad_k, grad_v = [], [], []
    for t in range(TILES):
        cut = slice(t * LANES, (t + 1) * LANES)
        upstream = two_heads(grad_context[:, cut])
        grad_p = mm_t(values[:, cut], upstream)
        grad_v.append(mm(probs_low[t], upstream).astype(BF16))
        inner = jnp.sum(grad_p * probs[t], axis=0, keepdims=True)
        grad_s = (probs[t] * (grad_p - inner) * scale).astype(BF16)
        grad_k.append(mm(grad_s, two_heads(query[:, cut])).astype(BF16))
        grad_q.append(tmm(stacked(grad_s), two_heads(keys[:, cut])).astype(BF16))
    grad_values = jnp.concatenate(grad_v, axis=1)
    grad_normed = (
        mm_t(jnp.concatenate(grad_q, axis=1), attn_ref[0])
        + mm_t(jnp.concatenate(grad_k, axis=1), attn_ref[1])
        + mm_t(grad_values, attn_ref[2])
    )
    grad_in = grad_mid + norm_backward(state_in, inv_in, grad_normed)
    grad_rows = grad_in.astype(BF16)
    rows_ref[...] = grad_rows
    rest = (grad_in - grad_rows.astype(F32)).astype(BF16)
    grad_embed = mm(in_hot, grad_rows) + mm(in_hot, rest)

    attn_cols = mm(normed_in, owner_columns(D, 3, core)).astype(BF16)
    attn_grad = tmm(attn_cols, grad_values)
    move = owner_columns(256, 4, core)
    tail = jnp.concatenate(
        [
            grad_table[:8],
            grad_table[8:],
            jnp.concatenate([loss, jnp.zeros((7, ROWS), F32)], axis=0),
            jnp.zeros((8, D - 3 * LANES), F32),
        ],
        axis=1,
    )
    small = (
        [grad_head[8 * b : 8 * b + 8] for b in range(4)]
        + [grad_embed[8 * b : 8 * b + 8] for b in range(4)]
        + [tail]
        + [jnp.zeros((8, D), F32)] * 7
    )
    for x in range(NX):
        pos_cols = mm(pos[:, 256 * x : 256 * x + 256], move).astype(BF16)
        proj_grad = tmm(pos_cols, grad_rows)
        for half, out in enumerate((send_ref, keep_ref)):
            for y in range(NY):
                a = 128 * half + 32 * y
                b = 192 * x + 96 * half + 24 * y
                out[NY * x + y] = jnp.concatenate(
                    [proj_grad[a : a + 32], attn_grad[b : b + 24], small[NY * x + y]], axis=0
                ).astype(BF16)


def plane_kernel(in_ref, out_ref):
    total = in_ref[0].astype(F32)
    for s in range(1, NX * NY):
        total = total + in_ref[s].astype(F32)
    pad = jnp.zeros((1, D), F32)
    for z in range(NZ):
        out_ref[z] = jnp.concatenate(
            [total[4 * z : 4 * z + 4], total[32 + 3 * z : 35 + 3 * z], pad, total[56:64]], axis=0
        ).astype(BF16)


def column_kernel(in_ref, proj_ref, attn_ref, small_ref):
    total = in_ref[0].astype(F32)
    for s in range(1, NZ):
        total = total + in_ref[s].astype(F32)
    proj_ref[...] = total[0:4]
    attn_ref[...] = total[4:7]
    mine = total[8:16].astype(BF16)
    for s in range(NX * NY // 2):
        small_ref[s] = jnp.concatenate([mine, mine], axis=0)


def last_kernel(in_ref, head_ref, embed_ref, table_ref, loss_ref):
    got = in_ref[...].astype(F32)
    head_ref[...] = jnp.transpose(got[0:32])
    embed_ref[...] = got[32:64]
    tail = got[64:72]
    table_ref[...] = jnp.concatenate([tail[:, 0:NIB], tail[:, LANES : LANES + NIB]], axis=0)
    loss_ref[...] = jnp.sum(tail[0:1, 2 * LANES : 3 * LANES], axis=1, keepdims=True) / TOTAL_BYTES


def call(kernel, outs, vmem=16 * 1024 * 1024):
    return pl.pallas_call(
        kernel,
        out_shape=[jax.ShapeDtypeStruct(s, d) for s, d in outs],
        compiler_params=pltpu.CompilerParams(vmem_limit_bytes=vmem),
    )


def local(
    global_out, in_nibbles, target_nibbles, proj_weight, attn_weight, head_weight, byte_embed, lo_table
):
    plane = ("x", "y")
    pos = lax.all_to_all(
        global_out.reshape(K, PD, DGT), ("y", "c"), split_axis=0, concat_axis=0, tiled=True
    ).reshape(ROWS, DGT)
    nibbles = jnp.concatenate([in_nibbles, target_nibbles], axis=0)
    nibbles = nibbles.transpose(0, 2, 1).reshape(4, ROWS)
    send, keep, grad_rows = call(
        main_kernel,
        [((16, BLK, D), BF16), ((16, BLK, D), BF16), ((ROWS, D), BF16)],
        48 * 1024 * 1024,
    )(pos, nibbles, proj_weight, attn_weight, head_weight.T, byte_embed, lo_table.T)
    got = lax.ppermute(send, "c", [(0, 1), (1, 0)])
    pair = (got.astype(F32) + keep.astype(F32)).astype(BF16)
    blocks = lax.all_to_all(pair, plane, split_axis=0, concat_axis=0, tiled=True)
    (columns,) = call(plane_kernel, [((NZ, 16, D), BF16)])(blocks)
    columns = lax.all_to_all(columns, "z", split_axis=0, concat_axis=0, tiled=True)
    grad_proj, grad_attn, small = call(
        column_kernel, [((4, D), F32), ((3, D), F32), ((NX * NY // 2, 16, D), BF16)]
    )(columns)
    small = lax.all_to_all(
        small.reshape(NX * NY, 8, D), plane, split_axis=0, concat_axis=0, tiled=True
    )
    grad_head, grad_embed, grad_table, loss = call(
        last_kernel,
        [((D, 2 * NIB), F32), ((2 * NIB, D), F32), ((NIB, NIB), F32), ((1, 1), F32)],
    )(small.reshape(NX * NY * 8, D))

    grad_back = lax.all_to_all(
        grad_rows.reshape(K, PD, D), ("y", "c"), split_axis=0, concat_axis=0, tiled=True
    ).reshape(ROWS, D)
    grad_global = mm_t(grad_back, proj_weight).astype(BF16)
    return (
        grad_global,
        grad_proj,
        grad_attn.reshape(3 * D),
        grad_head,
        grad_embed,
        grad_table,
        loss.reshape(()),
    )


def solution(mesh):
    axes = Mesh(mesh.devices.reshape(NX, NZ, NY, NC), ("x", "z", "y", "c"))
    every = ("x", "z", "y", "c")
    shard = P(("x", "z"), ("y", "c"))
    in_specs = (shard, P(None, every, None), P(None, every, None), P(), P(), P(), P(), P())
    out_specs = (shard, P(every, None), P(every), P(), P(), P(), P())
    return jax.shard_map(local, mesh=axes, in_specs=in_specs, out_specs=out_specs, check_vma=False)
```

time: 369 us -> 99.7 us (0.27)
  waiting for transfers between devices: 190 us -> 21.6 us
  blocking collectives: 81.2 us -> 44.6 us
  matrix products: 30.8 us -> 1.35 us
  local copies, waits for them, and re-layouts: 31.4 us -> 5.25 us
  between operations: 16.5 us -> 0.69 us
  Pallas kernels: 0 us -> 11.8 us
  other arithmetic: 6.51 us -> 1.2 us
    unnamed x2 -> x0, waiting for transfers between devices: 185 us -> none
    psum x1 -> x0, blocking collectives: 81.2 us -> none  [local(): lax.psum((loss_sum, part_head, part_embed, part_table), ('seq', 'tp'))]
    all_to_all x0 -> x2, blocking collectives: none -> 44.6 us  [the longest x1 27.8 us: local(): lax.all_to_all(pair, plane, split_axis=0, concat_axis=0, tiled=True)]
    dot_general x24 -> x1, matrix products: 29.2 us -> 1.35 us  [mm_t(): lax.dot_general(a, b, (((1,), (1,)), ((), ())), preferred_element_type=F32)]
    all_to_all x2 -> x3, waiting for transfers between devices: 4.88 us -> 18.2 us  [the longest x1 6.18 us: local(): lax.all_to_all(small.reshape(NX * NY, 8, D), plane, split_axis=0, concat_...]
    convert_element_type x8 -> x0, local copies, waits for them, and re-layouts: 12.5 us -> none  [to_low(): return lax.optimization_barrier(tensor.astype(jnp.bfloat16))]
    pallas_call x0 -> x4, Pallas kernels: none -> 11.8 us  [the longest x1 10.2 us: local(): call(main_kernel, [((16, BLK, D), BF16), ((16, BLK, D), BF16), ((ROWS, D)...]
    reshape x5 -> x2, local copies, waits for them, and re-layouts: 7.19 us -> 0.69 us  [the longest x1 0.61 us: local(): grad_attn.reshape(3 * D)]
  transfers between devices with their start and end apart: 3 -> 4, of which waited for: 2 -> 4; matrix products, arithmetic and copies ran while one was open for 1% -> 4% of each run, Pallas kernels for 0% -> 1%
where the time goes in v1:
time: 99.7 us; the launch traced here: 98 us
  blocking collectives  44.6 us (45%)
  waiting for transfers between devices  21.6 us (22%)
  Pallas kernels  11.8 us (12%)
  starting transfers between devices  11.5 us (12%)
  local copies, waits for them, and re-layouts  5.25 us (5%)
  matrix products  1.35 us (1%)
  other arithmetic  1.2 us (1%)
    all_to_all x1, blocking collectives, local(): lax.all_to_all(pair, plane, split_axis=0, concat_axis=0, tiled=True)  27.8 us
    all_to_all x1, blocking collectives, local(): lax.all_to_all(columns, 'z', split_axis=0, concat_axis=0, tiled=True)  16.8 us
    pallas_call x1, Pallas kernels, local(): call(main_kernel, [((16, BLK, D), BF16), ((16, BLK, D), BF16), ((ROWS, D)...  10.2 us
    all_to_all x1, waiting for transfers between devices, local(): lax.all_to_all(small.reshape(NX * NY, 8, D), plane, split_axis=0, concat_...  6.18 us
    all_to_all x1, waiting for transfers between devices, local(): lax.all_to_all(grad_rows.reshape(K, PD, D), ('y', 'c'), split_axis=0, con...  6.04 us
    all_to_all x1, waiting for transfers between devices, local(): lax.all_to_all(global_out.reshape(K, PD, DGT), ('y', 'c'), split_axis=0,...  5.97 us
    unnamed x10, local copies, waits for them, and re-layouts  4.56 us
    all_to_all x1, starting transfers between devices, local(): lax.all_to_all(global_out.reshape(K, PD, DGT), ('y', 'c'), split_axis=0,...  4.48 us
  transfers between devices with their start and end apart: 4, of which 4 were waited for; matrix products, arithmetic and copies ran while one was open for 4% of the time, Pallas kernels for 1%

profile of v1, /device:TPU:32, one launch (start us, length us, event | category | flops | bytes accessed | tf_op | source)
XLA Modules:
  0.0 98.0 jit_solution(11112200837512247493)
XLA Ops:
  0.6 4.5 %all-to-all-start = ((bf16[8,16,1024]{2,1,0:T(8,128)(2,1)}), bf16[8,16,1024]{2,1,0:T(8,128)(2,1)S(1)}, u32[]{:S(2)}, u32[]{:S(2)}) async-start(bf16[8,16,1024]{2,1,0:T(8,128)(2,1)} %bitcast.18), calls=%async_computation | async-start | bytes 524288 | tf_op jit(solution)/shard_map/all_to_all | solution.py:234
  5.1 0.7 add_bitcast_fusion
  5.8 0.1 reshape.43.nib_ref
  5.9 0.8 copy.15
  6.7 6.0 %all-to-all-done = bf16[8,16,1024]{2,1,0:T(8,128)(2,1)S(1)} async-done(((bf16[8,16,1024]{2,1,0:T(8,128)(2,1)}), bf16[8,16,1024]{2,1,0:T(8,128)(2,1)S(1)}, u32[]{:S(2)}, u32[]{:S(2)}) %all-to-all-start) | async-done | bytes 262176 | tf_op jit(solution)/shard_map/all_to_all | solution.py:234
  12.7 0.0 copy-start
  12.7 1.4 %copy-done = bf16[1024,768]{1,0:T(8,128)(2,1)S(1)} copy-done((bf16[1024,768]{1,0:T(8,128)(2,1)S(1)}, bf16[1024,768]{1,0:T(8,128)(2,1)}, u32[]{:S(2)}) %copy-start) | copy-done | bytes 1572888
  14.1 0.0 copy-start.2
  14.1 0.8 copy-done.2
  14.9 0.0 copy-start.3
  14.9 0.8 copy-done.3
  15.7 10.2 %shard_map.135 = (bf16[16,64,768]{2,1,0:T(8,128)(2,1)S(1)}, bf16[16,64,768]{2,1,0:T(8,128)(2,1)S(1)}, bf16[128,768]{1,0:T(8,128)(2,1)}) custom-call(bf16[128,1024]{1,0:T(8,128)(2,1)S(1)} %bitcast.13, s32[4,128]{1,0:T(4,128)S(1)} %reshape.43.nib_ref, bf16[1024,768]{1,0:T(8,128)(2,1)S(1)} %copy-done, bf16[4,768,768]{2,1,0:T(8,128)(2,1)} %attn_ref.1, ...), custom_call_target="tpu_custom_call" | custom-call | tf_op jit(solution)/shard_map/pallas_call | solution.py:239
  25.9 0.1 collective-permute-start
  26.0 3.4 %collective-permute-done = bf16[16,64,768]{2,1,0:T(8,128)(2,1)S(1)} collective-permute-done((bf16[16,64,768]{2,1,0:T(8,128)(2,1)S(1)}, bf16[16,64,768]{2,1,0:T(8,128)(2,1)S(1)}, u32[]{:S(2)}, u32[]{:S(2)}) %collective-permute-start) | collective-permute-done | bytes 1572896 | tf_op jit(solution)/shard_map/ppermute | solution.py:244
  29.4 0.5 add_convert_fusion
  29.9 27.8 %all_to_all.25.in_ref = bf16[16,64,768]{2,1,0:T(8,128)(2,1)S(1)} all-to-all(bf16[16,64,768]{2,1,0:T(8,128)(2,1)S(1)} %add_convert_fusion), channel_id=1, replica_groups=mesh['x'=4,'z'=8,'y'=4,'c'=2] {'x','y'}, dimensions={0} | all-to-all | bytes 3145728 | tf_op jit(solution)/shard_map/all_to_all | solution.py:246
  57.7 0.0 copy-start.1
  57.7 0.2 shard_map.136
  57.9 16.8 %all_to_all.26.in_ref = bf16[8,16,768]{2,1,0:T(8,128)(2,1)S(1)} all-to-all(bf16[8,16,768]{2,1,0:T(8,128)(2,1)S(1)} %shard_map.136), channel_id=1, replica_groups=mesh['x'=4,'z'=8,'y'=4,'c'=2] {'z'}, dimensions={0} | all-to-all | bytes 393216 | tf_op jit(solution)/shard_map/all_to_all | solution.py:248
  74.7 3.4 %all-to-all-start.1 = ((bf16[8,16,768]{2,1,0:T(8,128)(2,1)}), bf16[8,16,768]{2,1,0:T(8,128)(2,1)S(1)}, u32[]{:S(2)}, u32[]{:S(2)}) async-start(bf16[8,16,768]{2,1,0:T(8,128)(2,1)} %bitcast.5), calls=%async_computation.1 | async-start | bytes 393216 | tf_op jit(solution)/shard_map/all_to_all | solution.py:260
  78.1 0.7 shard_map.137
  78.9 6.0 %all-to-all-done.1 = bf16[8,16,768]{2,1,0:T(8,128)(2,1)S(1)} async-done(((bf16[8,16,768]{2,1,0:T(8,128)(2,1)}), bf16[8,16,768]{2,1,0:T(8,128)(2,1)S(1)}, u32[]{:S(2)}, u32[]{:S(2)}) %all-to-all-start.1) | async-done | bytes 196640 | tf_op jit(solution)/shard_map/all_to_all | solution.py:260
  84.9 3.5 %all-to-all-start.4 = ((bf16[16,8,768]{2,1,0:T(8,128)(2,1)}), bf16[16,8,768]{2,1,0:T(8,128)(2,1)S(1)}, u32[]{:S(2)}, u32[]{:S(2)}) async-start(bf16[16,8,768]{2,1,0:T(8,128)(2,1)} %bitcast.7), calls=%async_computation.4 | async-start | bytes 393216 | tf_op jit(solution)/shard_map/all_to_all | solution.py:252
  88.4 0.0 copy-done.1
  88.4 1.3 %convolution_convert_fusion = bf16[128,1024]{1,0:T(8,128)(2,1)} fusion(bf16[128,768]{1,0:T(8,128)(2,1)S(1)} %bitcast.17, bf16[1024,768]{1,0:T(8,128)(2,1)S(1)} %copy-done.1), kind=kOutput, calls=%fused_computation.1 | convolution fusion | flops 201457664 | bytes 2031616 | tf_op jit(solution)/shard_map/dot_general | solution.py:31
  89.8 0.6 reshape.46
  90.4 6.2 %all-to-all-done.4 = bf16[16,8,768]{2,1,0:T(8,128)(2,1)S(1)} async-done(((bf16[16,8,768]{2,1,0:T(8,128)(2,1)}), bf16[16,8,768]{2,1,0:T(8,128)(2,1)S(1)}, u32[]{:S(2)}, u32[]{:S(2)}) %all-to-all-start.4) | async-done | bytes 196640 | tf_op jit(solution)/shard_map/all_to_all | solution.py:252
  96.6 0.7 shard_map.138
  97.2 0.8 copy.16
Async XLA Ops:
  0.6 12.0 %all-to-all-start = ((bf16[8,16,1024]{2,1,0:T(8,128)(2,1)}), bf16[8,16,1024]{2,1,0:T(8,128)(2,1)S(1)}, u32[]{:S(2)}, u32[]{:S(2)}) async-start(bf16[8,16,1024]{2,1,0:T(8,128)(2,1)} %bitcast.18), calls=%async_computation | async-start | bytes 524288 | tf_op jit(solution)/shard_map/all_to_all | solution.py:234
  12.7 1.4 %copy-start = (bf16[1024,768]{1,0:T(8,128)(2,1)S(1)}, bf16[1024,768]{1,0:T(8,128)(2,1)}, u32[]{:S(2)}) copy-start(bf16[1024,768]{1,0:T(8,128)(2,1)} %proj_ref.1) | copy-start | bytes 4718596
  14.1 0.8 copy-start.2
  14.9 0.8 copy-start.3
  25.9 3.5 %collective-permute-start = (bf16[16,64,768]{2,1,0:T(8,128)(2,1)S(1)}, bf16[16,64,768]{2,1,0:T(8,128)(2,1)S(1)}, u32[]{:S(2)}, u32[]{:S(2)}) collective-permute-start(bf16[16,64,768]{2,1,0:T(8,128)(2,1)S(1)} %get-tuple-element.18), channel_id=1, source_target_pairs={{0,1},{1,0},{2,3},{3,2},{4,5},{5,4},{6,7},{7,6},{8,9},{9,8},{10,11... | collective-permute-start | bytes 4718600 | tf_op jit(solution)/shard_map/ppermute | solution.py:244
  57.7 30.7 %copy-start.1 = (bf16[1024,768]{1,0:T(8,128)(2,1)S(1)}, bf16[1024,768]{1,0:T(8,128)(2,1)}, u32[]{:S(2)}) copy-start(bf16[1024,768]{1,0:T(8,128)(2,1)} %proj_ref.1) | copy-start | bytes 4718596
  74.7 10.2 %all-to-all-start.1 = ((bf16[8,16,768]{2,1,0:T(8,128)(2,1)}), bf16[8,16,768]{2,1,0:T(8,128)(2,1)S(1)}, u32[]{:S(2)}, u32[]{:S(2)}) async-start(bf16[8,16,768]{2,1,0:T(8,128)(2,1)} %bitcast.5), calls=%async_computation.1 | async-start | bytes 393216 | tf_op jit(solution)/shard_map/all_to_all | solution.py:260
  84.9 11.7 %all-to-all-start.4 = ((bf16[16,8,768]{2,1,0:T(8,128)(2,1)}), bf16[16,8,768]{2,1,0:T(8,128)(2,1)S(1)}, u32[]{:S(2)}, u32[]{:S(2)}) async-start(bf16[16,8,768]{2,1,0:T(8,128)(2,1)} %bitcast.7), calls=%async_computation.4 | async-start | bytes 393216 | tf_op jit(solution)/shard_map/all_to_all | solution.py:252

commit v2 on v1

--- a/solution.py
+++ b/solution.py
@@ -19,7 +19,10 @@
 F32 = jnp.float32
 BF16 = jnp.bfloat16
 NX, NZ, NY, NC = 4, 8, 4, 2
-BLK = 64
+PLANE = NX * NY
+SMALL = 512
+BLK = 7 * D + SMALL
+GROWS = 336
 TOTAL_BYTES = 32768
 
 
@@ -45,11 +48,11 @@
 def owner_columns(size, piece, core):
     block = NZ * NY * NC * piece
     src = lax.broadcasted_iota(jnp.int32, (size, size), 0)
-    dst = lax.broadcasted_iota(jnp.int32, (size, size), 1)
-    xb = dst // block
-    w = dst - xb * block
-    half = w // (block // 2)
-    w = w - half * (block // 2)
+    dst = lax.broadcasted_iota(jnp.int32, (1, size), 1)
+    half = dst // (size // 2)
+    w = dst - half * (size // 2)
+    xb = w // (block // 2)
+    w = w - xb * (block // 2)
     y = w // (NZ * piece)
     w = w - y * (NZ * piece)
     z = w // piece
@@ -70,19 +73,54 @@
     return top + jnp.log(total) - jnp.sum(logits * onehot, axis=0, keepdims=True)
 
 
+def fetch_kernel(proj_hbm, proj_ref, sem):
+    copy = pltpu.make_async_copy(proj_hbm, proj_ref, sem)
+    copy.start()
+    copy.wait()
+
+
+def input_hot(nib_ref):
+    codes = lax.broadcasted_iota(jnp.int32, (2 * NIB, ROWS), 0)
+    return jnp.logical_or(codes == nib_ref[0:1, :], codes == nib_ref[1:2, :] + NIB).astype(BF16)
+
+
 def main_kernel(
-    pos_ref, nib_ref, proj_ref, attn_ref, head_ref, embed_ref, lo_ref, send_ref, keep_ref, rows_ref
+    pos_ref,
+    nib_ref,
+    proj_ref,
+    embed_ref,
+    attn_hbm,
+    head_ref,
+    lo_ref,
+    out_ref,
+    send_ref,
+    keep_ref,
+    attn_ref,
+    sems,
 ):
+    copies = [pltpu.make_async_copy(attn_hbm.at[w], attn_ref.at[w], sems.at[w]) for w in range(4)]
+    for copy in copies:
+        copy.start()
     core = lax.axis_index("c")
     pos = pos_ref[...]
     projected = mm(pos, proj_ref[...]).astype(BF16).astype(F32)
-    codes = lax.broadcasted_iota(jnp.int32, (2 * NIB, ROWS), 0)
-    in_hot = jnp.logical_or(codes == nib_ref[0:1, :], codes == nib_ref[1:2, :] + NIB).astype(BF16)
+    in_hot = input_hot(nib_ref)
     state_in = projected + tmm(in_hot, embed_ref[...])
     inv_in = lax.rsqrt(jnp.mean(state_in * state_in, axis=-1, keepdims=True) + EPS)
     normed_in = (state_in * inv_in).astype(BF16)
+    move = owner_columns(256, 4, core)
+    for x in range(NX):
+        cols = mm(pos[:, 256 * x : 256 * x + 256], move).astype(BF16)
+        send_ref[:, 128 * x : 128 * x + 128] = cols[:, :128]
+        keep_ref[:, 128 * x : 128 * x + 128] = cols[:, 128:]
+    cols = mm(normed_in, owner_columns(D, 3, core)).astype(BF16)
+    send_ref[:, 512:] = cols[:, : D // 2]
+    keep_ref[:, 512:] = cols[:, D // 2 :]
+    copies[0].wait()
     query = mm(normed_in, attn_ref[0]).astype(BF16)
+    copies[1].wait()
     keys = mm(normed_in, attn_ref[1]).astype(BF16)
+    copies[2].wait()
     values = mm(normed_in, attn_ref[2]).astype(BF16)
 
     key_row = lax.broadcasted_iota(jnp.int32, (ROWS, 2 * ROWS), 0)
@@ -109,6 +147,7 @@
         probs_low.append(low)
         contexts.append(tmm(stacked(low), two_heads(values[:, cut])).astype(BF16))
     context = jnp.concatenate(contexts, axis=1)
+    copies[3].wait()
     state_mid = state_in + mm(context, attn_ref[3])
     inv_mid = lax.rsqrt(jnp.mean(state_mid * state_mid, axis=-1, keepdims=True) + EPS)
     normed_mid = (state_mid * inv_mid).astype(BF16)
@@ -154,13 +193,11 @@
     )
     grad_in = grad_mid + norm_backward(state_in, inv_in, grad_normed)
     grad_rows = grad_in.astype(BF16)
-    rows_ref[...] = grad_rows
     rest = (grad_in - grad_rows.astype(F32)).astype(BF16)
     grad_embed = mm(in_hot, grad_rows) + mm(in_hot, rest)
 
-    attn_cols = mm(normed_in, owner_columns(D, 3, core)).astype(BF16)
-    attn_grad = tmm(attn_cols, grad_values)
-    move = owner_columns(256, 4, core)
+    out_ref[0:ROWS] = grad_rows
+    out_ref[ROWS : 2 * ROWS] = grad_values
     tail = jnp.concatenate(
         [
             grad_table[:8],
@@ -170,60 +207,86 @@
         ],
         axis=1,
     )
-    small = (
-        [grad_head[8 * b : 8 * b + 8] for b in range(4)]
-        + [grad_embed[8 * b : 8 * b + 8] for b in range(4)]
-        + [tail]
-        + [jnp.zeros((8, D), F32)] * 7
-    )
-    for x in range(NX):
-        pos_cols = mm(pos[:, 256 * x : 256 * x + 256], move).astype(BF16)
-        proj_grad = tmm(pos_cols, grad_rows)
-        for half, out in enumerate((send_ref, keep_ref)):
-            for y in range(NY):
-                a = 128 * half + 32 * y
-                b = 192 * x + 96 * half + 24 * y
-                out[NY * x + y] = jnp.concatenate(
-                    [proj_grad[a : a + 32], attn_grad[b : b + 24], small[NY * x + y]], axis=0
-                ).astype(BF16)
+    out_ref[2 * ROWS : GROWS] = jnp.concatenate(
+        [grad_head, grad_embed, tail, jnp.zeros((8, D), F32)], axis=0
+    ).astype(BF16)
+
+
+def pair_kernel(ka_ref, ra_ref, kg_ref, rg_ref, out_ref, *back_refs):
+    core = lax.axis_index("c")
+    y = lax.axis_index("y")
+    cols = jnp.concatenate([ka_ref[...], ra_ref[...]], axis=0)
+    rows = jnp.concatenate([kg_ref[0:ROWS], rg_ref[0:ROWS]], axis=0)
+    values = jnp.concatenate([kg_ref[ROWS : 2 * ROWS], rg_ref[ROWS : 2 * ROWS]], axis=0)
+    for d, back in enumerate(back_refs):
+        at = pl.ds(pl.multiple_of((2 * lax.rem(y + d, NY) + core) * PD, PD), PD)
+        mine, other = kg_ref[at], rg_ref[at]
+        first = core == 0
+        back[0:PD] = jnp.where(first, mine, other)
+        back[PD : 2 * PD] = jnp.where(first, other, mine)
+    small = kg_ref[2 * ROWS :].astype(F32) + rg_ref[2 * ROWS :].astype(F32)
+    flat = jnp.concatenate(
+        [small[8 * g : 8 * g + 8] for g in range(9)] + [jnp.zeros((8, PLANE * SMALL - 9 * D), F32)], axis=1
+    ).astype(BF16)
+    proj_grad = tmm(cols[:, :512], rows)
+    attn_grad = tmm(cols[:, 512:], values)
+    for b in range(PLANE):
+        groups = [proj_grad[32 * b + 8 * g : 32 * b + 8 * g + 8] for g in range(4)]
+        groups += [attn_grad[24 * b + 8 * g : 24 * b + 8 * g + 8] for g in range(3)]
+        for g, group in enumerate(groups):
+            out_ref[b, :, g * D : (g + 1) * D] = group.astype(BF16)
+        out_ref[b, :, 7 * D :] = flat[:, b * SMALL : (b + 1) * SMALL]
+
+
+def back_kernel(p0_ref, p1_ref, p2_ref, p3_ref, proj_ref, out_ref, rows_ref):
+    y = lax.axis_index("y")
+    for d, piece in enumerate((p0_ref, p1_ref, p2_ref, p3_ref)):
+        at = pl.ds(pl.multiple_of(lax.rem(y - d + NY, NY) * 2 * PD, 2 * PD), 2 * PD)
+        rows_ref[at] = piece[...]
+    out_ref[...] = mm_t(rows_ref[...], proj_ref[...]).astype(BF16)
 
 
 def plane_kernel(in_ref, out_ref):
     total = in_ref[0].astype(F32)
-    for s in range(1, NX * NY):
+    for s in range(1, PLANE):
         total = total + in_ref[s].astype(F32)
+    proj = jnp.concatenate([total[:, g * D : (g + 1) * D] for g in range(4)], axis=0)
+    attn = jnp.concatenate([total[:, g * D : (g + 1) * D] for g in range(4, 7)], axis=0)
+    small = total[:, 7 * D :].astype(BF16)
     pad = jnp.zeros((1, D), F32)
     for z in range(NZ):
-        out_ref[z] = jnp.concatenate(
-            [total[4 * z : 4 * z + 4], total[32 + 3 * z : 35 + 3 * z], pad, total[56:64]], axis=0
-        ).astype(BF16)
+        own = jnp.concatenate([proj[4 * z : 4 * z + 4], attn[3 * z : 3 * z + 3], pad], axis=0)
+        out_ref[z, :, :D] = own.astype(BF16)
+        out_ref[z, :, D:] = small
 
 
 def column_kernel(in_ref, proj_ref, attn_ref, small_ref):
     total = in_ref[0].astype(F32)
     for s in range(1, NZ):
         total = total + in_ref[s].astype(F32)
-    proj_ref[...] = total[0:4]
-    attn_ref[...] = total[4:7]
-    mine = total[8:16].astype(BF16)
-    for s in range(NX * NY // 2):
-        small_ref[s] = jnp.concatenate([mine, mine], axis=0)
+    proj_ref[...] = total[0:4, :D]
+    attn_ref[...] = total[4:7, :D]
+    mine = total[:, D:].astype(BF16)
+    for s in range(PLANE):
+        small_ref[s] = mine
 
 
 def last_kernel(in_ref, head_ref, embed_ref, table_ref, loss_ref):
-    got = in_ref[...].astype(F32)
-    head_ref[...] = jnp.transpose(got[0:32])
-    embed_ref[...] = got[32:64]
-    tail = got[64:72]
+    got = jnp.concatenate([in_ref[b] for b in range(13)], axis=1).astype(F32)
+    for g in range(4):
+        head_ref[8 * g : 8 * g + 8] = got[:, g * D : (g + 1) * D]
+        embed_ref[8 * g : 8 * g + 8] = got[:, (4 + g) * D : (5 + g) * D]
+    tail = got[:, 8 * D :]
     table_ref[...] = jnp.concatenate([tail[:, 0:NIB], tail[:, LANES : LANES + NIB]], axis=0)
     loss_ref[...] = jnp.sum(tail[0:1, 2 * LANES : 3 * LANES], axis=1, keepdims=True) / TOTAL_BYTES
 
 
-def call(kernel, outs, vmem=16 * 1024 * 1024):
+def call(kernel, outs, vmem=8, **more):
     return pl.pallas_call(
         kernel,
         out_shape=[jax.ShapeDtypeStruct(s, d) for s, d in outs],
-        compiler_params=pltpu.CompilerParams(vmem_limit_bytes=vmem),
+        compiler_params=pltpu.CompilerParams(vmem_limit_bytes=vmem * 1024 * 1024),
+        **more,
     )
 
 
@@ -231,41 +294,54 @@
     global_out, in_nibbles, target_nibbles, proj_weight, attn_weight, head_weight, byte_embed, lo_table
 ):
     plane = ("x", "y")
+    swap = [(0, 1), (1, 0)]
     pos = lax.all_to_all(
         global_out.reshape(K, PD, DGT), ("y", "c"), split_axis=0, concat_axis=0, tiled=True
     ).reshape(ROWS, DGT)
     nibbles = jnp.concatenate([in_nibbles, target_nibbles], axis=0)
     nibbles = nibbles.transpose(0, 2, 1).reshape(4, ROWS)
-    send, keep, grad_rows = call(
+    (proj_weight,) = call(
+        fetch_kernel,
+        [(proj_weight.shape, BF16)],
+        in_specs=[pl.BlockSpec(memory_space=pl.ANY)],
+        scratch_shapes=[pltpu.SemaphoreType.DMA],
+    )(proj_weight)
+    half = (ROWS, (DGT + D) // NC)
+    local_spec = pl.BlockSpec(memory_space=pltpu.VMEM)
+    grads, send_cols, keep_cols = call(
         main_kernel,
-        [((16, BLK, D), BF16), ((16, BLK, D), BF16), ((ROWS, D), BF16)],
-        48 * 1024 * 1024,
-    )(pos, nibbles, proj_weight, attn_weight, head_weight.T, byte_embed, lo_table.T)
-    got = lax.ppermute(send, "c", [(0, 1), (1, 0)])
-    pair = (got.astype(F32) + keep.astype(F32)).astype(BF16)
-    blocks = lax.all_to_all(pair, plane, split_axis=0, concat_axis=0, tiled=True)
-    (columns,) = call(plane_kernel, [((NZ, 16, D), BF16)])(blocks)
+        [((GROWS, D), BF16), (half, BF16), (half, BF16)],
+        52,
+        in_specs=[local_spec] * 4 + [pl.BlockSpec(memory_space=pl.ANY)] + [local_spec] * 2,
+        scratch_shapes=[pltpu.VMEM((4, D, D), BF16), pltpu.SemaphoreType.DMA((4,))],
+    )(pos, nibbles, proj_weight, byte_embed, attn_weight, head_weight.T, lo_table.T)
+    got_cols = lax.ppermute(send_cols, "c", swap)
+    got_grads = lax.ppermute(grads, "c", swap)
+    blocks, *back = call(pair_kernel, [((PLANE, 8, BLK), BF16)] + [((2 * PD, D), BF16)] * NY, 12)(
+        keep_cols, got_cols, grads, got_grads
+    )
+    blocks = lax.all_to_all(blocks, plane, split_axis=0, concat_axis=0, tiled=True)
+    for d in range(1, NY):
+        back[d] = lax.ppermute(back[d], "y", [(s, (s + d) % NY) for s in range(NY)])
+    (grad_global,) = call(
+        back_kernel, [((ROWS, DGT), BF16)], scratch_shapes=[pltpu.VMEM((ROWS, D), BF16)]
+    )(*back, proj_weight)
+    blocks, grad_global = lax.optimization_barrier((blocks, grad_global))
+    (columns,) = call(plane_kernel, [((NZ, 8, D + SMALL), BF16)])(blocks)
     columns = lax.all_to_all(columns, "z", split_axis=0, concat_axis=0, tiled=True)
     grad_proj, grad_attn, small = call(
-        column_kernel, [((4, D), F32), ((3, D), F32), ((NX * NY // 2, 16, D), BF16)]
+        column_kernel, [((4, D), F32), ((3, D), F32), ((PLANE, 8, SMALL), BF16)]
     )(columns)
-    small = lax.all_to_all(
-        small.reshape(NX * NY, 8, D), plane, split_axis=0, concat_axis=0, tiled=True
-    )
-    grad_head, grad_embed, grad_table, loss = call(
+    small = lax.all_to_all(small, plane, split_axis=0, concat_axis=0, tiled=True)
+    head_rows, grad_embed, grad_table, loss = call(
         last_kernel,
-        [((D, 2 * NIB), F32), ((2 * NIB, D), F32), ((NIB, NIB), F32), ((1, 1), F32)],
-    )(small.reshape(NX * NY * 8, D))
-
-    grad_back = lax.all_to_all(
-        grad_rows.reshape(K, PD, D), ("y", "c"), split_axis=0, concat_axis=0, tiled=True
-    ).reshape(ROWS, D)
-    grad_global = mm_t(grad_back, proj_weight).astype(BF16)
+        [((2 * NIB, D), F32), ((2 * NIB, D), F32), ((NIB, NIB), F32), ((1, 1), F32)],
+    )(small)
     return (
         grad_global,
         grad_proj,
         grad_attn.reshape(3 * D),
-        grad_head,
+        head_rows.T,
         grad_embed,
         grad_table,
         loss.reshape(()),

time: 99.7 us -> 86.3 us (0.87)
  blocking collectives: 44.6 us -> 16.3 us
  starting transfers between devices: 11.5 us -> 21.9 us
  waiting for transfers between devices: 21.6 us -> 29.7 us
  matrix products: 1.35 us -> 0 us
  other arithmetic: 1.2 us -> 0.01 us
    all_to_all x1 -> x0, blocking collectives: 27.8 us -> none  [local(): lax.all_to_all(pair, plane, split_axis=0, concat_axis=0, tiled=True)]
    ppermute x1 -> x5, waiting for transfers between devices: 3.4 us -> 16.6 us  [the longest x3 14.9 us: local(): back[d] = lax.ppermute(back[d], 'y', [(s, (s + d) % NY) for s in range(NY)])]
    ppermute x1 -> x5, starting transfers between devices: 0.09 us -> 6.65 us  [the longest x3 6.06 us: local(): back[d] = lax.ppermute(back[d], 'y', [(s, (s + d) % NY) for s in range(NY)])]
    all_to_all x2, starting transfers between devices: 6.91 us -> 10.8 us  [the longest x1 5.63 us: local(): lax.all_to_all(small, plane, split_axis=0, concat_axis=0, tiled=True)]
    all_to_all x2, waiting for transfers between devices: 12.2 us -> 8.41 us  [the longest x1 7.23 us: local(): lax.all_to_all(small, plane, split_axis=0, concat_axis=0, tiled=True)]
    dot_general x1 -> x0, matrix products: 1.35 us -> none  [mm_t(): lax.dot_general(a, b, (((1,), (1,)), ((), ())), preferred_element_type=F32)]
    all_to_all x1, waiting for transfers between devices: 5.97 us -> 4.65 us  [local(): lax.all_to_all(global_out.reshape(K, PD, DGT), ('y', 'c'), split_axis=0,...]
    unnamed x10 -> x19, local copies, waits for them, and re-layouts: 4.56 us -> 3.76 us
  transfers between devices with their start and end apart: 4 -> 8, of which waited for: 4 -> 5; matrix products, arithmetic and copies ran while one was open for 4% -> 1% of each run, Pallas kernels for 1% -> 2%
where the time goes in v2:
time: 86.3 us; the launch traced here: 85.5 us
  waiting for transfers between devices  29.7 us (34%)
  starting transfers between devices  21.9 us (25%)
  blocking collectives  16.3 us (19%)
  Pallas kernels  12.3 us (14%)
  local copies, waits for them, and re-layouts  4.45 us (5%)
    all_to_all x1, blocking collectives, local(): lax.all_to_all(columns, 'z', split_axis=0, concat_axis=0, tiled=True)  16.3 us
    ppermute x3, waiting for transfers between devices, local(): back[d] = lax.ppermute(back[d], 'y', [(s, (s + d) % NY) for s in range(NY)])  14.9 us
    pallas_call x1, Pallas kernels, local(): call(main_kernel, [((GROWS, D), BF16), (half, BF16), (half, BF16)], 52, i...  8.73 us
    all_to_all x1, waiting for transfers between devices, local(): lax.all_to_all(small, plane, split_axis=0, concat_axis=0, tiled=True)  7.23 us
    ppermute x3, starting transfers between devices, local(): back[d] = lax.ppermute(back[d], 'y', [(s, (s + d) % NY) for s in range(NY)])  6.06 us
    all_to_all x1, starting transfers between devices, local(): lax.all_to_all(small, plane, split_axis=0, concat_axis=0, tiled=True)  5.63 us
    all_to_all x1, starting transfers between devices, local(): lax.all_to_all(blocks, plane, split_axis=0, concat_axis=0, tiled=True)  5.13 us
    all_to_all x1, waiting for transfers between devices, local(): lax.all_to_all(global_out.reshape(K, PD, DGT), ('y', 'c'), split_axis=0,...  4.65 us
  transfers between devices with their start and end apart: 8, of which 5 were waited for; matrix products, arithmetic and copies ran while one was open for 1% of the time, Pallas kernels for 2%

profile of v2, /device:TPU:32, one launch (start us, length us, event | category | flops | bytes accessed | tf_op | source)
XLA Modules:
  0.0 85.5 jit_solution(4040963909667301981)
XLA Ops:
  0.6 4.5 %all-to-all-start = ((bf16[8,16,1024]{2,1,0:T(8,128)(2,1)}), bf16[8,16,1024]{2,1,0:T(8,128)(2,1)S(1)}, u32[]{:S(2)}, u32[]{:S(2)}) async-start(bf16[8,16,1024]{2,1,0:T(8,128)(2,1)} %bitcast.11), calls=%async_computation | async-start | bytes 524288 | tf_op jit(solution)/shard_map/all_to_all | solution.py:298
  5.1 0.0 copy-start.2
  5.1 1.4 %copy-done.2 = bf16[1024,768]{1,0:T(8,128)(2,1)S(1)} copy-done((bf16[1024,768]{1,0:T(8,128)(2,1)S(1)}, bf16[1024,768]{1,0:T(8,128)(2,1)}, u32[]{:S(2)}) %copy-start.2) | copy-done | bytes 1572888
  6.5 0.0 copy-start.7
  6.5 0.0 copy-start.8
  6.5 0.0 copy-start.6
  6.5 0.0 copy-start.4
  6.5 0.0 copy-start.5
  6.5 0.1 shard_map.135.proj_ref
  6.7 0.0 copy-start
  6.7 1.2 %copy-done = bf16[1024,768]{1,0:T(8,128)(2,1)} copy-done((bf16[1024,768]{1,0:T(8,128)(2,1)}, bf16[1024,768]{1,0:T(8,128)(2,1)S(1)}, u32[]{:S(2)}) %copy-start) | copy-done | bytes 1572888
  7.8 0.0 copy-done.7
  7.8 0.0 copy-done.8
  7.8 0.1 reshape.31.nib_ref
  7.9 0.0 copy-done.6
  7.9 0.1 copy.15
  8.0 4.7 %all-to-all-done = bf16[8,16,1024]{2,1,0:T(8,128)(2,1)S(1)} async-done(((bf16[8,16,1024]{2,1,0:T(8,128)(2,1)}), bf16[8,16,1024]{2,1,0:T(8,128)(2,1)S(1)}, u32[]{:S(2)}, u32[]{:S(2)}) %all-to-all-start) | async-done | bytes 262176 | tf_op jit(solution)/shard_map/all_to_all | solution.py:298
  12.7 0.0 copy-done.4
  12.7 0.0 copy-done.5
  12.7 8.7 %shard_map.136 = (bf16[336,768]{1,0:T(8,128)(2,1)S(1)}, bf16[128,896]{1,0:T(8,128)(2,1)S(1)}, bf16[128,896]{1,0:T(8,128)(2,1)S(1)}) custom-call(bf16[128,1024]{1,0:T(8,128)(2,1)S(1)} %bitcast.8, s32[4,128]{1,0:T(4,128)S(1)} %reshape.31.nib_ref, bf16[1024,768]{1,0:T(8,128)(2,1)} %copy-done, bf16[32,768]{1,0:T(8,128)(2,1)S(1)} %copy-done.4, ...), custom_call_target="tpu_custom_call" | custom-call | tf_op jit(solution)/shard_map/pallas_call | solution.py:311
  21.4 0.1 collective-permute-start.1
  21.5 0.5 collective-permute-start
  22.0 1.7 %collective-permute-done.ra_ref = bf16[128,896]{1,0:T(8,128)(2,1)S(1)} collective-permute-done((bf16[128,896]{1,0:T(8,128)(2,1)S(1)}, bf16[128,896]{1,0:T(8,128)(2,1)S(1)}, u32[]{:S(2)}, u32[]{:S(2)}) %collective-permute-start) | collective-permute-done | bytes 229408 | tf_op jit(solution)/shard_map/ppermute | solution.py:318
  23.7 0.0 collective-permute-done.1.rg_ref
  23.7 0.6 shard_map.137
  24.3 0.0 copy-start.3
  24.3 1.1 %copy-done.3 = bf16[16,8,5888]{2,1,0:T(8,128)(2,1)} copy-done((bf16[16,8,5888]{2,1,0:T(8,128)(2,1)}, bf16[16,8,5888]{2,1,0:T(8,128)(2,1)S(1)}, u32[]{:S(2)}) %copy-start.3) | copy-done | bytes 1507352
  25.4 0.0 copy-start.1
  25.4 5.1 %all-to-all-start.1 = ((bf16[16,8,5888]{2,1,0:T(8,128)(2,1)}), bf16[16,8,5888]{2,1,0:T(8,128)(2,1)S(1)}, u32[]{:S(2)}, u32[]{:S(2)}) async-start(bf16[16,8,5888]{2,1,0:T(8,128)(2,1)} %copy-done.3), calls=%async_computation.1 | async-start | bytes 3014656 | tf_op jit(solution)/shard_map/all_to_all | solution.py:323
  30.5 1.9 %collective-permute-start.2 = (bf16[32,768]{1,0:T(8,128)(2,1)S(1)}, bf16[32,768]{1,0:T(8,128)(2,1)S(1)}, u32[]{:S(2)}, u32[]{:S(2)}) collective-permute-start(bf16[32,768]{1,0:T(8,128)(2,1)S(1)} %get-tuple-element.29), channel_id=1, source_target_pairs={{0,2},{2,4},{4,6},{6,0},{1,3},{3,5},{5,7},{7,1},{8,10},{10,12},{12... | collective-permute-start | bytes 147464 | tf_op jit(solution)/shard_map/ppermute | solution.py:325
  32.5 2.7 %collective-permute-start.3 = (bf16[32,768]{1,0:T(8,128)(2,1)S(1)}, bf16[32,768]{1,0:T(8,128)(2,1)S(1)}, u32[]{:S(2)}, u32[]{:S(2)}) collective-permute-start(bf16[32,768]{1,0:T(8,128)(2,1)S(1)} %get-tuple-element.30), channel_id=1, source_target_pairs={{0,4},{2,6},{4,0},{6,2},{1,5},{3,7},{5,1},{7,3},{8,12},{10,14},{12... | collective-permute-start | bytes 147464 | tf_op jit(solution)/shard_map/ppermute | solution.py:325
  35.1 1.5 %collective-permute-start.4 = (bf16[32,768]{1,0:T(8,128)(2,1)S(1)}, bf16[32,768]{1,0:T(8,128)(2,1)S(1)}, u32[]{:S(2)}, u32[]{:S(2)}) collective-permute-start(bf16[32,768]{1,0:T(8,128)(2,1)S(1)} %get-tuple-element.31), channel_id=1, source_target_pairs={{0,6},{2,0},{4,2},{6,4},{1,7},{3,1},{5,3},{7,5},{8,14},{10,8},{12,... | collective-permute-start | bytes 147464 | tf_op jit(solution)/shard_map/ppermute | solution.py:325
  36.6 14.9 %collective-permute-done.2.p1_ref = bf16[32,768]{1,0:T(8,128)(2,1)S(1)} collective-permute-done((bf16[32,768]{1,0:T(8,128)(2,1)S(1)}, bf16[32,768]{1,0:T(8,128)(2,1)S(1)}, u32[]{:S(2)}, u32[]{:S(2)}) %collective-permute-start.2) | collective-permute-done | bytes 49184 | tf_op jit(solution)/shard_map/ppermute | solution.py:325
  51.5 0.0 collective-permute-done.3.p2_ref
  51.5 0.0 collective-permute-done.4.p3_ref
  51.5 0.0 copy-done.1
  51.5 1.3 %shard_map.138 = bf16[128,1024]{1,0:T(8,128)(2,1)} custom-call(bf16[32,768]{1,0:T(8,128)(2,1)S(1)} %get-tuple-element.28.p0_ref, bf16[32,768]{1,0:T(8,128)(2,1)S(1)} %collective-permute-done.2.p1_ref, bf16[32,768]{1,0:T(8,128)(2,1)S(1)} %collective-permute-done.3.p2_ref, bf16[32,768]{1,0:T(8,128)(2,1)S(1)} %collective-permute-done.4.p3_ref, ...), custom_call_target="tpu_custom_call" | custom-call | tf_op jit(solution)/shard_map/pallas_call | solution.py:326
  52.9 1.2 %all-to-all-done.1.in_ref = bf16[16,8,5888]{2,1,0:T(8,128)(2,1)S(1)} async-done(((bf16[16,8,5888]{2,1,0:T(8,128)(2,1)}), bf16[16,8,5888]{2,1,0:T(8,128)(2,1)S(1)}, u32[]{:S(2)}, u32[]{:S(2)}) %all-to-all-start.1) | async-done | bytes 1507360 | tf_op jit(solution)/shard_map/all_to_all | solution.py:323
  54.1 0.2 shard_map.139
  54.3 16.3 %all_to_all.20.in_ref = bf16[8,8,1280]{2,1,0:T(8,128)(2,1)S(1)} all-to-all(bf16[8,8,1280]{2,1,0:T(8,128)(2,1)S(1)} %shard_map.139), channel_id=1, replica_groups=mesh['x'=4,'z'=8,'y'=4,'c'=2] {'z'}, dimensions={0} | all-to-all | bytes 327680 | tf_op jit(solution)/shard_map/all_to_all | solution.py:331
  70.6 0.7 shard_map.140
  71.3 5.6 %all-to-all-start.3 = ((bf16[16,8,512]{2,1,0:T(8,128)(2,1)}), bf16[16,8,512]{2,1,0:T(8,128)(2,1)S(1)}, u32[]{:S(2)}, u32[]{:S(2)}) async-start(bf16[16,8,512]{2,1,0:T(8,128)(2,1)} %get-tuple-element.36), calls=%async_computation.3 | async-start | bytes 262144 | tf_op jit(solution)/shard_map/all_to_all | solution.py:335
  76.9 0.6 reshape.32
  77.6 7.2 %all-to-all-done.3.in_ref = bf16[16,8,512]{2,1,0:T(8,128)(2,1)S(1)} async-done(((bf16[16,8,512]{2,1,0:T(8,128)(2,1)}), bf16[16,8,512]{2,1,0:T(8,128)(2,1)S(1)}, u32[]{:S(2)}, u32[]{:S(2)}) %all-to-all-start.3) | async-done | bytes 131104 | tf_op jit(solution)/shard_map/all_to_all | solution.py:335
  84.8 0.7 shard_map.141
  (1 shorter events, 0.0 us)
Async XLA Ops:
  0.6 12.0 %all-to-all-start = ((bf16[8,16,1024]{2,1,0:T(8,128)(2,1)}), bf16[8,16,1024]{2,1,0:T(8,128)(2,1)S(1)}, u32[]{:S(2)}, u32[]{:S(2)}) async-start(bf16[8,16,1024]{2,1,0:T(8,128)(2,1)} %bitcast.11), calls=%async_computation | async-start | bytes 524288 | tf_op jit(solution)/shard_map/all_to_all | solution.py:298
  5.1 1.4 %copy-start.2 = (bf16[1024,768]{1,0:T(8,128)(2,1)S(1)}, bf16[1024,768]{1,0:T(8,128)(2,1)}, u32[]{:S(2)}) copy-start(bf16[1024,768]{1,0:T(8,128)(2,1)} %proj_hbm.1) | copy-start | bytes 4718596
  6.5 1.3 %copy-start.7 = (s32[2,16,8]{1,2,0:T(8,128)S(1)}, s32[2,16,8]{1,2,0:T(8,128)}, u32[]{:S(2)}) copy-start(s32[2,16,8]{1,2,0:T(8,128)} %param.10) | copy-start | bytes 3076
  6.5 1.3 %copy-start.8 = (s32[2,16,8]{1,2,0:T(8,128)S(1)}, s32[2,16,8]{1,2,0:T(8,128)}, u32[]{:S(2)}) copy-start(s32[2,16,8]{1,2,0:T(8,128)} %param.9) | copy-start | bytes 3076
  6.5 1.4 %copy-start.6 = (f32[16,16]{1,0:T(8,128)S(1)}, f32[16,16]{1,0:T(8,128)}, u32[]{:S(2)}) copy-start(f32[16,16]{1,0:T(8,128)} %param.15) | copy-start | bytes 3076
  6.5 6.1 %copy-start.4 = (bf16[32,768]{1,0:T(8,128)(2,1)S(1)}, bf16[32,768]{1,0:T(8,128)(2,1)}, u32[]{:S(2)}) copy-start(bf16[32,768]{1,0:T(8,128)(2,1)} %embed_ref.1) | copy-start | bytes 147460
  6.5 6.1 %copy-start.5 = (bf16[768,32]{0,1:T(8,128)(2,1)S(1)}, bf16[768,32]{0,1:T(8,128)(2,1)}, u32[]{:S(2)}) copy-start(bf16[768,32]{0,1:T(8,128)(2,1)} %param.13) | copy-start | bytes 147460
  6.7 1.2 %copy-start = (bf16[1024,768]{1,0:T(8,128)(2,1)}, bf16[1024,768]{1,0:T(8,128)(2,1)S(1)}, u32[]{:S(2)}) copy-start(bf16[1024,768]{1,0:T(8,128)(2,1)S(1)} %shard_map.135.proj_ref) | copy-start | bytes 4718596
  21.4 2.3 %collective-permute-start.1 = (bf16[336,768]{1,0:T(8,128)(2,1)S(1)}, bf16[336,768]{1,0:T(8,128)(2,1)S(1)}, u32[]{:S(2)}, u32[]{:S(2)}) collective-permute-start(bf16[336,768]{1,0:T(8,128)(2,1)S(1)} %get-tuple-element.26.kg_ref), channel_id=1, source_target_pairs={{0,1},{1,0},{2,3},{3,2},{4,5},{5,4},{6,7},{7,6},{8,9},{9,8},{10,11... | collective-permute-start | bytes 1548296 | tf_op jit(solution)/shard_map/ppermute | solution.py:319
  21.5 2.2 %collective-permute-start = (bf16[128,896]{1,0:T(8,128)(2,1)S(1)}, bf16[128,896]{1,0:T(8,128)(2,1)S(1)}, u32[]{:S(2)}, u32[]{:S(2)}) collective-permute-start(bf16[128,896]{1,0:T(8,128)(2,1)S(1)} %get-tuple-element.25), channel_id=1, source_target_pairs={{0,1},{1,0},{2,3},{3,2},{4,5},{5,4},{6,7},{7,6},{8,9},{9,8},{10,11... | collective-permute-start | bytes 688136 | tf_op jit(solution)/shard_map/ppermute | solution.py:318
  24.3 1.1 %copy-start.3 = (bf16[16,8,5888]{2,1,0:T(8,128)(2,1)}, bf16[16,8,5888]{2,1,0:T(8,128)(2,1)S(1)}, u32[]{:S(2)}) copy-start(bf16[16,8,5888]{2,1,0:T(8,128)(2,1)S(1)} %get-tuple-element.27) | copy-start | bytes 4521988
  25.4 26.1 %copy-start.1 = (bf16[1024,768]{1,0:T(8,128)(2,1)S(1)}, bf16[1024,768]{1,0:T(8,128)(2,1)}, u32[]{:S(2)}) copy-start(bf16[1024,768]{1,0:T(8,128)(2,1)} %copy-done) | copy-start | bytes 4718596
  25.4 28.7 %all-to-all-start.1 = ((bf16[16,8,5888]{2,1,0:T(8,128)(2,1)}), bf16[16,8,5888]{2,1,0:T(8,128)(2,1)S(1)}, u32[]{:S(2)}, u32[]{:S(2)}) async-start(bf16[16,8,5888]{2,1,0:T(8,128)(2,1)} %copy-done.3), calls=%async_computation.1 | async-start | bytes 3014656 | tf_op jit(solution)/shard_map/all_to_all | solution.py:323
  30.5 21.0 %collective-permute-start.2 = (bf16[32,768]{1,0:T(8,128)(2,1)S(1)}, bf16[32,768]{1,0:T(8,128)(2,1)S(1)}, u32[]{:S(2)}, u32[]{:S(2)}) collective-permute-start(bf16[32,768]{1,0:T(8,128)(2,1)S(1)} %get-tuple-element.29), channel_id=1, source_target_pairs={{0,2},{2,4},{4,6},{6,0},{1,3},{3,5},{5,7},{7,1},{8,10},{10,12},{12... | collective-permute-start | bytes 147464 | tf_op jit(solution)/shard_map/ppermute | solution.py:325
  32.5 19.1 %collective-permute-start.3 = (bf16[32,768]{1,0:T(8,128)(2,1)S(1)}, bf16[32,768]{1,0:T(8,128)(2,1)S(1)}, u32[]{:S(2)}, u32[]{:S(2)}) collective-permute-start(bf16[32,768]{1,0:T(8,128)(2,1)S(1)} %get-tuple-element.30), channel_id=1, source_target_pairs={{0,4},{2,6},{4,0},{6,2},{1,5},{3,7},{5,1},{7,3},{8,12},{10,14},{12... | collective-permute-start | bytes 147464 | tf_op jit(solution)/shard_map/ppermute | solution.py:325
  35.1 16.4 %collective-permute-start.4 = (bf16[32,768]{1,0:T(8,128)(2,1)S(1)}, bf16[32,768]{1,0:T(8,128)(2,1)S(1)}, u32[]{:S(2)}, u32[]{:S(2)}) collective-permute-start(bf16[32,768]{1,0:T(8,128)(2,1)S(1)} %get-tuple-element.31), channel_id=1, source_target_pairs={{0,6},{2,0},{4,2},{6,4},{1,7},{3,1},{5,3},{7,5},{8,14},{10,8},{12,... | collective-permute-start | bytes 147464 | tf_op jit(solution)/shard_map/ppermute | solution.py:325
  71.3 13.5 %all-to-all-start.3 = ((bf16[16,8,512]{2,1,0:T(8,128)(2,1)}), bf16[16,8,512]{2,1,0:T(8,128)(2,1)S(1)}, u32[]{:S(2)}, u32[]{:S(2)}) async-start(bf16[16,8,512]{2,1,0:T(8,128)(2,1)} %get-tuple-element.36), calls=%async_computation.3 | async-start | bytes 262144 | tf_op jit(solution)/shard_map/all_to_all | solution.py:335

commit v3 on v2

--- a/solution.py
+++ b/solution.py
@@ -321,14 +321,15 @@
         keep_cols, got_cols, grads, got_grads
     )
     blocks = lax.all_to_all(blocks, plane, split_axis=0, concat_axis=0, tiled=True)
+    (columns,) = call(plane_kernel, [((NZ, 8, D + SMALL), BF16)])(blocks)
+    columns, *back = lax.optimization_barrier((columns, *back))
+    columns = lax.all_to_all(columns, "z", split_axis=0, concat_axis=0, tiled=True)
     for d in range(1, NY):
         back[d] = lax.ppermute(back[d], "y", [(s, (s + d) % NY) for s in range(NY)])
     (grad_global,) = call(
         back_kernel, [((ROWS, DGT), BF16)], scratch_shapes=[pltpu.VMEM((ROWS, D), BF16)]
     )(*back, proj_weight)
-    blocks, grad_global = lax.optimization_barrier((blocks, grad_global))
-    (columns,) = call(plane_kernel, [((NZ, 8, D + SMALL), BF16)])(blocks)
-    columns = lax.all_to_all(columns, "z", split_axis=0, concat_axis=0, tiled=True)
+    columns, grad_global = lax.optimization_barrier((columns, grad_global))
     grad_proj, grad_attn, small = call(
         column_kernel, [((4, D), F32), ((3, D), F32), ((PLANE, 8, SMALL), BF16)]
     )(columns)

time: 86.3 us -> 83.4 us (0.966)
  waiting for transfers between devices: 29.7 us -> 15.1 us
  blocking collectives: 16.3 us -> 27.1 us
    ppermute x3, waiting for transfers between devices: 14.9 us -> 2.89 us  [local(): back[d] = lax.ppermute(back[d], 'y', [(s, (s + d) % NY) for s in range(NY)])]
    all_to_all x1, blocking collectives: 16.3 us -> 27.1 us  [local(): lax.all_to_all(blocks, plane, split_axis=0, concat_axis=0, tiled=True)]
    all_to_all x1, starting transfers between devices: 5.13 us -> 8.57 us  [local(): lax.all_to_all(columns, 'z', split_axis=0, concat_axis=0, tiled=True)]
    ppermute x3, starting transfers between devices: 6.06 us -> 3.79 us  [local(): back[d] = lax.ppermute(back[d], 'y', [(s, (s + d) % NY) for s in range(NY)])]
    all_to_all x1, waiting for transfers between devices: 4.65 us -> 3.25 us  [local(): lax.all_to_all(global_out.reshape(K, PD, DGT), ('y', 'c'), split_axis=0,...]
    all_to_all x1, waiting for transfers between devices: 1.17 us -> 0.01 us  [local(): lax.all_to_all(columns, 'z', split_axis=0, concat_axis=0, tiled=True)]
    all_to_all x1, starting transfers between devices: 5.63 us -> 4.74 us  [local(): lax.all_to_all(small, plane, split_axis=0, concat_axis=0, tiled=True)]
    unnamed x19 -> x11, local copies, waits for them, and re-layouts: 3.76 us -> 3.36 us
  transfers between devices with their start and end apart: 8 -> 8, of which waited for: 5 -> 6; matrix products, arithmetic and copies ran while one was open for 1% -> 3% of each run, Pallas kernels for 2% -> 2%
where the time goes in v3:
time: 83.4 us; the launch traced here: 82.9 us
  blocking collectives  27.1 us (32%)
  starting transfers between devices  22.2 us (27%)
  waiting for transfers between devices  15.1 us (18%)
  Pallas kernels  13 us (16%)
  local copies, waits for them, and re-layouts  4.05 us (5%)
    all_to_all x1, blocking collectives, local(): lax.all_to_all(blocks, plane, split_axis=0, concat_axis=0, tiled=True)  27.1 us
    pallas_call x1, Pallas kernels, local(): call(main_kernel, [((GROWS, D), BF16), (half, BF16), (half, BF16)], 52, i...  8.73 us
    all_to_all x1, starting transfers between devices, local(): lax.all_to_all(columns, 'z', split_axis=0, concat_axis=0, tiled=True)  8.57 us
    all_to_all x1, waiting for transfers between devices, local(): lax.all_to_all(small, plane, split_axis=0, concat_axis=0, tiled=True)  7.23 us
    all_to_all x1, starting transfers between devices, local(): lax.all_to_all(small, plane, split_axis=0, concat_axis=0, tiled=True)  4.74 us
    all_to_all x1, starting transfers between devices, local(): lax.all_to_all(global_out.reshape(K, PD, DGT), ('y', 'c'), split_axis=0,...  4.48 us
    ppermute x3, starting transfers between devices, local(): back[d] = lax.ppermute(back[d], 'y', [(s, (s + d) % NY) for s in range(NY)])  3.79 us
    unnamed x11, local copies, waits for them, and re-layouts  3.36 us
  transfers between devices with their start and end apart: 8, of which 6 were waited for; matrix products, arithmetic and copies ran while one was open for 3% of the time, Pallas kernels for 2%

profile of v3, /device:TPU:32, one launch (start us, length us, event | category | flops | bytes accessed | tf_op | source)
XLA Modules:
  0.0 82.9 jit_solution(5268831287873181291)
XLA Ops:
  0.6 4.5 %all-to-all-start = ((bf16[8,16,1024]{2,1,0:T(8,128)(2,1)}), bf16[8,16,1024]{2,1,0:T(8,128)(2,1)S(1)}, u32[]{:S(2)}, u32[]{:S(2)}) async-start(bf16[8,16,1024]{2,1,0:T(8,128)(2,1)} %bitcast.11), calls=%async_computation | async-start | bytes 524288 | tf_op jit(solution)/shard_map/all_to_all | solution.py:298
  5.1 0.8 copy.15
  5.9 0.7 add_bitcast_fusion
  6.6 0.1 reshape.31.nib_ref
  6.7 0.0 copy-start.2
  6.7 1.4 %copy-done.2 = bf16[1024,768]{1,0:T(8,128)(2,1)S(1)} copy-done((bf16[1024,768]{1,0:T(8,128)(2,1)S(1)}, bf16[1024,768]{1,0:T(8,128)(2,1)}, u32[]{:S(2)}) %copy-start.2) | copy-done | bytes 1572888
  8.1 0.0 copy-start.3
  8.1 0.0 copy-start.4
  8.1 0.1 shard_map.135.proj_ref
  8.2 0.0 copy-start
  8.2 1.2 %copy-done = bf16[1024,768]{1,0:T(8,128)(2,1)} copy-done((bf16[1024,768]{1,0:T(8,128)(2,1)}, bf16[1024,768]{1,0:T(8,128)(2,1)S(1)}, u32[]{:S(2)}) %copy-start) | copy-done | bytes 1572888
  9.4 3.3 %all-to-all-done = bf16[8,16,1024]{2,1,0:T(8,128)(2,1)S(1)} async-done(((bf16[8,16,1024]{2,1,0:T(8,128)(2,1)}), bf16[8,16,1024]{2,1,0:T(8,128)(2,1)S(1)}, u32[]{:S(2)}, u32[]{:S(2)}) %all-to-all-start) | async-done | bytes 262176 | tf_op jit(solution)/shard_map/all_to_all | solution.py:298
  12.7 0.0 copy-done.3
  12.7 0.0 copy-done.4
  12.7 8.7 %shard_map.136 = (bf16[336,768]{1,0:T(8,128)(2,1)S(1)}, bf16[128,896]{1,0:T(8,128)(2,1)S(1)}, bf16[128,896]{1,0:T(8,128)(2,1)S(1)}) custom-call(bf16[128,1024]{1,0:T(8,128)(2,1)S(1)} %bitcast.8, s32[4,128]{1,0:T(4,128)S(1)} %reshape.31.nib_ref, bf16[1024,768]{1,0:T(8,128)(2,1)} %copy-done, bf16[32,768]{1,0:T(8,128)(2,1)S(1)} %copy-done.3, ...), custom_call_target="tpu_custom_call" | custom-call | tf_op jit(solution)/shard_map/pallas_call | solution.py:311
  21.4 0.1 collective-permute-start.1
  21.5 0.5 collective-permute-start
  22.0 1.7 %collective-permute-done.ra_ref = bf16[128,896]{1,0:T(8,128)(2,1)S(1)} collective-permute-done((bf16[128,896]{1,0:T(8,128)(2,1)S(1)}, bf16[128,896]{1,0:T(8,128)(2,1)S(1)}, u32[]{:S(2)}, u32[]{:S(2)}) %collective-permute-start) | collective-permute-done | bytes 229408 | tf_op jit(solution)/shard_map/ppermute | solution.py:318
  23.7 0.0 collective-permute-done.1.rg_ref
  23.7 0.6 shard_map.137
  24.3 27.1 %all_to_all.20.in_ref = bf16[16,8,5888]{2,1,0:T(8,128)(2,1)S(1)} all-to-all(bf16[16,8,5888]{2,1,0:T(8,128)(2,1)S(1)} %get-tuple-element.32), channel_id=1, replica_groups=mesh['x'=4,'z'=8,'y'=4,'c'=2] {'x','y'}, dimensions={0} | all-to-all | bytes 3014656 | tf_op jit(solution)/shard_map/all_to_all | solution.py:323
  51.4 0.0 copy-start.1
  51.4 0.9 %shard_map.138 = bf16[8,8,1280]{2,1,0:T(8,128)(2,1)} custom-call(bf16[16,8,5888]{2,1,0:T(8,128)(2,1)S(1)} %all_to_all.20.in_ref), custom_call_target="tpu_custom_call" | custom-call | tf_op jit(solution)/shard_map/pallas_call | solution.py:324
  52.3 8.6 %all-to-all-start.2 = ((bf16[8,8,1280]{2,1,0:T(8,128)(2,1)}), bf16[8,8,1280]{2,1,0:T(8,128)(2,1)S(1)}, u32[]{:S(2)}, u32[]{:S(2)}) async-start(bf16[8,8,1280]{2,1,0:T(8,128)(2,1)} %shard_map.138), calls=%async_computation.2 | async-start | bytes 327680 | tf_op jit(solution)/shard_map/all_to_all | solution.py:326
  60.9 0.6 collective-permute-start.2
  61.4 1.5 %collective-permute-start.3 = (bf16[32,768]{1,0:T(8,128)(2,1)S(1)}, bf16[32,768]{1,0:T(8,128)(2,1)S(1)}, u32[]{:S(2)}, u32[]{:S(2)}) collective-permute-start(bf16[32,768]{1,0:T(8,128)(2,1)S(1)} %get-tuple-element.40), channel_id=1, source_target_pairs={{0,4},{2,6},{4,0},{6,2},{1,5},{3,7},{5,1},{7,3},{8,12},{10,14},{12... | collective-permute-start | bytes 147464 | tf_op jit(solution)/shard_map/ppermute | solution.py:328
  62.9 1.8 %collective-permute-start.4 = (bf16[32,768]{1,0:T(8,128)(2,1)S(1)}, bf16[32,768]{1,0:T(8,128)(2,1)S(1)}, u32[]{:S(2)}, u32[]{:S(2)}) collective-permute-start(bf16[32,768]{1,0:T(8,128)(2,1)S(1)} %get-tuple-element.41), channel_id=1, source_target_pairs={{0,6},{2,0},{4,2},{6,4},{1,7},{3,1},{5,3},{7,5},{8,14},{10,8},{12,... | collective-permute-start | bytes 147464 | tf_op jit(solution)/shard_map/ppermute | solution.py:328
  64.7 1.5 %collective-permute-done.2.p1_ref = bf16[32,768]{1,0:T(8,128)(2,1)S(1)} collective-permute-done((bf16[32,768]{1,0:T(8,128)(2,1)S(1)}, bf16[32,768]{1,0:T(8,128)(2,1)S(1)}, u32[]{:S(2)}, u32[]{:S(2)}) %collective-permute-start.2) | collective-permute-done | bytes 49184 | tf_op jit(solution)/shard_map/ppermute | solution.py:328
  66.2 0.9 %collective-permute-done.3.p2_ref = bf16[32,768]{1,0:T(8,128)(2,1)S(1)} collective-permute-done((bf16[32,768]{1,0:T(8,128)(2,1)S(1)}, bf16[32,768]{1,0:T(8,128)(2,1)S(1)}, u32[]{:S(2)}, u32[]{:S(2)}) %collective-permute-start.3) | collective-permute-done | bytes 49184 | tf_op jit(solution)/shard_map/ppermute | solution.py:328
  67.0 0.5 collective-permute-done.4.p3_ref
  67.6 0.0 copy-done.1
  67.6 1.3 %shard_map.139 = bf16[128,1024]{1,0:T(8,128)(2,1)} custom-call(bf16[32,768]{1,0:T(8,128)(2,1)S(1)} %get-tuple-element.38.p0_ref, bf16[32,768]{1,0:T(8,128)(2,1)S(1)} %collective-permute-done.2.p1_ref, bf16[32,768]{1,0:T(8,128)(2,1)S(1)} %collective-permute-done.3.p2_ref, bf16[32,768]{1,0:T(8,128)(2,1)S(1)} %collective-permute-done.4.p3_ref, ...), custom_call_target="tpu_custom_call" | custom-call | tf_op jit(solution)/shard_map/pallas_call | solution.py:329
  68.9 0.0 all-to-all-done.2.in_ref
  68.9 0.7 shard_map.140
  69.6 4.7 %all-to-all-start.3 = ((bf16[16,8,512]{2,1,0:T(8,128)(2,1)}), bf16[16,8,512]{2,1,0:T(8,128)(2,1)S(1)}, u32[]{:S(2)}, u32[]{:S(2)}) async-start(bf16[16,8,512]{2,1,0:T(8,128)(2,1)} %get-tuple-element.46), calls=%async_computation.3 | async-start | bytes 262144 | tf_op jit(solution)/shard_map/all_to_all | solution.py:336
  74.3 0.6 reshape.32
  75.0 7.2 %all-to-all-done.3.in_ref = bf16[16,8,512]{2,1,0:T(8,128)(2,1)S(1)} async-done(((bf16[16,8,512]{2,1,0:T(8,128)(2,1)}), bf16[16,8,512]{2,1,0:T(8,128)(2,1)S(1)}, u32[]{:S(2)}, u32[]{:S(2)}) %all-to-all-start.3) | async-done | bytes 131104 | tf_op jit(solution)/shard_map/all_to_all | solution.py:336
  82.2 0.7 shard_map.141
Async XLA Ops:
  0.6 12.0 %all-to-all-start = ((bf16[8,16,1024]{2,1,0:T(8,128)(2,1)}), bf16[8,16,1024]{2,1,0:T(8,128)(2,1)S(1)}, u32[]{:S(2)}, u32[]{:S(2)}) async-start(bf16[8,16,1024]{2,1,0:T(8,128)(2,1)} %bitcast.11), calls=%async_computation | async-start | bytes 524288 | tf_op jit(solution)/shard_map/all_to_all | solution.py:298
  6.7 1.4 %copy-start.2 = (bf16[1024,768]{1,0:T(8,128)(2,1)S(1)}, bf16[1024,768]{1,0:T(8,128)(2,1)}, u32[]{:S(2)}) copy-start(bf16[1024,768]{1,0:T(8,128)(2,1)} %proj_hbm.1) | copy-start | bytes 4718596
  8.1 4.6 %copy-start.3 = (bf16[32,768]{1,0:T(8,128)(2,1)S(1)}, bf16[32,768]{1,0:T(8,128)(2,1)}, u32[]{:S(2)}) copy-start(bf16[32,768]{1,0:T(8,128)(2,1)} %embed_ref.1) | copy-start | bytes 147460
  8.1 4.6 %copy-start.4 = (bf16[768,32]{0,1:T(8,128)(2,1)S(1)}, bf16[768,32]{0,1:T(8,128)(2,1)}, u32[]{:S(2)}) copy-start(bf16[768,32]{0,1:T(8,128)(2,1)} %param.13) | copy-start | bytes 147460
  8.2 1.2 %copy-start = (bf16[1024,768]{1,0:T(8,128)(2,1)}, bf16[1024,768]{1,0:T(8,128)(2,1)S(1)}, u32[]{:S(2)}) copy-start(bf16[1024,768]{1,0:T(8,128)(2,1)S(1)} %shard_map.135.proj_ref) | copy-start | bytes 4718596
  21.4 2.3 %collective-permute-start.1 = (bf16[336,768]{1,0:T(8,128)(2,1)S(1)}, bf16[336,768]{1,0:T(8,128)(2,1)S(1)}, u32[]{:S(2)}, u32[]{:S(2)}) collective-permute-start(bf16[336,768]{1,0:T(8,128)(2,1)S(1)} %get-tuple-element.31.kg_ref), channel_id=1, source_target_pairs={{0,1},{1,0},{2,3},{3,2},{4,5},{5,4},{6,7},{7,6},{8,9},{9,8},{10,11... | collective-permute-start | bytes 1548296 | tf_op jit(solution)/shard_map/ppermute | solution.py:319
  21.5 2.2 %collective-permute-start = (bf16[128,896]{1,0:T(8,128)(2,1)S(1)}, bf16[128,896]{1,0:T(8,128)(2,1)S(1)}, u32[]{:S(2)}, u32[]{:S(2)}) collective-permute-start(bf16[128,896]{1,0:T(8,128)(2,1)S(1)} %get-tuple-element.30), channel_id=1, source_target_pairs={{0,1},{1,0},{2,3},{3,2},{4,5},{5,4},{6,7},{7,6},{8,9},{9,8},{10,11... | collective-permute-start | bytes 688136 | tf_op jit(solution)/shard_map/ppermute | solution.py:318
  51.4 16.1 %copy-start.1 = (bf16[1024,768]{1,0:T(8,128)(2,1)S(1)}, bf16[1024,768]{1,0:T(8,128)(2,1)}, u32[]{:S(2)}) copy-start(bf16[1024,768]{1,0:T(8,128)(2,1)} %copy-done) | copy-start | bytes 4718596
  52.3 16.6 %all-to-all-start.2 = ((bf16[8,8,1280]{2,1,0:T(8,128)(2,1)}), bf16[8,8,1280]{2,1,0:T(8,128)(2,1)S(1)}, u32[]{:S(2)}, u32[]{:S(2)}) async-start(bf16[8,8,1280]{2,1,0:T(8,128)(2,1)} %shard_map.138), calls=%async_computation.2 | async-start | bytes 327680 | tf_op jit(solution)/shard_map/all_to_all | solution.py:326
  60.9 5.3 %collective-permute-start.2 = (bf16[32,768]{1,0:T(8,128)(2,1)S(1)}, bf16[32,768]{1,0:T(8,128)(2,1)S(1)}, u32[]{:S(2)}, u32[]{:S(2)}) collective-permute-start(bf16[32,768]{1,0:T(8,128)(2,1)S(1)} %get-tuple-element.39), channel_id=1, source_target_pairs={{0,2},{2,4},{4,6},{6,0},{1,3},{3,5},{5,7},{7,1},{8,10},{10,12},{12... | collective-permute-start | bytes 147464 | tf_op jit(solution)/shard_map/ppermute | solution.py:328
  61.4 5.6 %collective-permute-start.3 = (bf16[32,768]{1,0:T(8,128)(2,1)S(1)}, bf16[32,768]{1,0:T(8,128)(2,1)S(1)}, u32[]{:S(2)}, u32[]{:S(2)}) collective-permute-start(bf16[32,768]{1,0:T(8,128)(2,1)S(1)} %get-tuple-element.40), channel_id=1, source_target_pairs={{0,4},{2,6},{4,0},{6,2},{1,5},{3,7},{5,1},{7,3},{8,12},{10,14},{12... | collective-permute-start | bytes 147464 | tf_op jit(solution)/shard_map/ppermute | solution.py:328
  62.9 4.7 %collective-permute-start.4 = (bf16[32,768]{1,0:T(8,128)(2,1)S(1)}, bf16[32,768]{1,0:T(8,128)(2,1)S(1)}, u32[]{:S(2)}, u32[]{:S(2)}) collective-permute-start(bf16[32,768]{1,0:T(8,128)(2,1)S(1)} %get-tuple-element.41), channel_id=1, source_target_pairs={{0,6},{2,0},{4,2},{6,4},{1,7},{3,1},{5,3},{7,5},{8,14},{10,8},{12,... | collective-permute-start | bytes 147464 | tf_op jit(solution)/shard_map/ppermute | solution.py:328
  69.6 12.6 %all-to-all-start.3 = ((bf16[16,8,512]{2,1,0:T(8,128)(2,1)}), bf16[16,8,512]{2,1,0:T(8,128)(2,1)S(1)}, u32[]{:S(2)}, u32[]{:S(2)}) async-start(bf16[16,8,512]{2,1,0:T(8,128)(2,1)} %get-tuple-element.46), calls=%async_computation.3 | async-start | bytes 262144 | tf_op jit(solution)/shard_map/all_to_all | solution.py:336

commit v4 on v3

--- a/solution.py
+++ b/solution.py
@@ -311,7 +311,7 @@
     grads, send_cols, keep_cols = call(
         main_kernel,
         [((GROWS, D), BF16), (half, BF16), (half, BF16)],
-        52,
+        50,
         in_specs=[local_spec] * 4 + [pl.BlockSpec(memory_space=pl.ANY)] + [local_spec] * 2,
         scratch_shapes=[pltpu.VMEM((4, D, D), BF16), pltpu.SemaphoreType.DMA((4,))],
     )(pos, nibbles, proj_weight, byte_embed, attn_weight, head_weight.T, lo_table.T)

time: 83.4 us -> 82 us (0.983)
  Pallas kernels: 13 us -> 11.6 us
  waiting for transfers between devices: 15.1 us -> 16.3 us
  local copies, waits for them, and re-layouts: 4.05 us -> 2.87 us
    pallas_call x1, Pallas kernels: 8.73 us -> 7.32 us  [local(): call(main_kernel, [((GROWS, D), BF16), (half, BF16), (half, BF16)], 50, i...]
    all_to_all x1, waiting for transfers between devices: 3.25 us -> 4.43 us  [local(): lax.all_to_all(global_out.reshape(K, PD, DGT), ('y', 'c'), split_axis=0,...]
    unnamed x11 -> x7, local copies, waits for them, and re-layouts: 3.36 us -> 2.18 us
where the time goes in v4:
time: 82 us; the launch traced here: 81.5 us
  blocking collectives  27.1 us (33%)
  starting transfers between devices  22.2 us (27%)
  waiting for transfers between devices  16.3 us (20%)
  Pallas kernels  11.6 us (14%)
  local copies, waits for them, and re-layouts  2.87 us (4%)
    all_to_all x1, blocking collectives, local(): lax.all_to_all(blocks, plane, split_axis=0, concat_axis=0, tiled=True)  27.1 us
    all_to_all x1, starting transfers between devices, local(): lax.all_to_all(columns, 'z', split_axis=0, concat_axis=0, tiled=True)  8.57 us
    pallas_call x1, Pallas kernels, local(): call(main_kernel, [((GROWS, D), BF16), (half, BF16), (half, BF16)], 50, i...  7.32 us
    all_to_all x1, waiting for transfers between devices, local(): lax.all_to_all(small, plane, split_axis=0, concat_axis=0, tiled=True)  7.23 us
    all_to_all x1, starting transfers between devices, local(): lax.all_to_all(small, plane, split_axis=0, concat_axis=0, tiled=True)  4.74 us
    all_to_all x1, starting transfers between devices, local(): lax.all_to_all(global_out.reshape(K, PD, DGT), ('y', 'c'), split_axis=0,...  4.48 us
    all_to_all x1, waiting for transfers between devices, local(): lax.all_to_all(global_out.reshape(K, PD, DGT), ('y', 'c'), split_axis=0,...  4.43 us
    ppermute x3, starting transfers between devices, local(): back[d] = lax.ppermute(back[d], 'y', [(s, (s + d) % NY) for s in range(NY)])  3.79 us
  transfers between devices with their start and end apart: 8, of which 6 were waited for; matrix products, arithmetic and copies ran while one was open for 3% of the time, Pallas kernels for 2%

profile of v4, /device:TPU:32, one launch (start us, length us, event | category | flops | bytes accessed | tf_op | source)
XLA Modules:
  0.0 81.5 jit_solution(9319461220285758833)
XLA Ops:
  0.6 4.5 %all-to-all-start = ((bf16[8,16,1024]{2,1,0:T(8,128)(2,1)}), bf16[8,16,1024]{2,1,0:T(8,128)(2,1)S(1)}, u32[]{:S(2)}, u32[]{:S(2)}) async-start(bf16[8,16,1024]{2,1,0:T(8,128)(2,1)} %bitcast.11), calls=%async_computation | async-start | bytes 524288 | tf_op jit(solution)/shard_map/all_to_all | solution.py:298
  5.1 0.8 copy.15
  5.9 0.7 add_bitcast_fusion
  6.6 0.1 reshape.31.nib_ref
  6.7 0.0 copy-start
  6.7 1.4 %copy-done = bf16[1024,768]{1,0:T(8,128)(2,1)S(1)} copy-done((bf16[1024,768]{1,0:T(8,128)(2,1)S(1)}, bf16[1024,768]{1,0:T(8,128)(2,1)}, u32[]{:S(2)}) %copy-start) | copy-done | bytes 1572888
  8.1 0.0 copy-start.1
  8.1 0.0 copy-start.2
  8.1 0.1 shard_map.135.proj_ref
  8.2 4.4 %all-to-all-done = bf16[8,16,1024]{2,1,0:T(8,128)(2,1)S(1)} async-done(((bf16[8,16,1024]{2,1,0:T(8,128)(2,1)}), bf16[8,16,1024]{2,1,0:T(8,128)(2,1)S(1)}, u32[]{:S(2)}, u32[]{:S(2)}) %all-to-all-start) | async-done | bytes 262176 | tf_op jit(solution)/shard_map/all_to_all | solution.py:298
  12.7 0.0 copy-done.1
  12.7 0.0 copy-done.2
  12.7 7.3 %shard_map.136 = (bf16[336,768]{1,0:T(8,128)(2,1)S(1)}, bf16[128,896]{1,0:T(8,128)(2,1)S(1)}, bf16[128,896]{1,0:T(8,128)(2,1)S(1)}) custom-call(bf16[128,1024]{1,0:T(8,128)(2,1)S(1)} %bitcast.8, s32[4,128]{1,0:T(4,128)S(1)} %reshape.31.nib_ref, bf16[1024,768]{1,0:T(8,128)(2,1)S(1)} %shard_map.135.proj_ref, bf16[32,768]{1,0:T(8,128)(2,1)S(1)} %copy-done.1, ...), custom_call_target="tpu_custom_call" | custom-call | tf_op jit(solution)/shard_map/pallas_call | solution.py:311
  20.0 0.1 collective-permute-start.1
  20.1 0.5 collective-permute-start
  20.6 1.7 %collective-permute-done.ra_ref = bf16[128,896]{1,0:T(8,128)(2,1)S(1)} collective-permute-done((bf16[128,896]{1,0:T(8,128)(2,1)S(1)}, bf16[128,896]{1,0:T(8,128)(2,1)S(1)}, u32[]{:S(2)}, u32[]{:S(2)}) %collective-permute-start) | collective-permute-done | bytes 229408 | tf_op jit(solution)/shard_map/ppermute | solution.py:318
  22.3 0.0 collective-permute-done.1.rg_ref
  22.3 0.6 shard_map.137
  22.9 27.1 %all_to_all.20.in_ref = bf16[16,8,5888]{2,1,0:T(8,128)(2,1)S(1)} all-to-all(bf16[16,8,5888]{2,1,0:T(8,128)(2,1)S(1)} %get-tuple-element.32), channel_id=1, replica_groups=mesh['x'=4,'z'=8,'y'=4,'c'=2] {'x','y'}, dimensions={0} | all-to-all | bytes 3014656 | tf_op jit(solution)/shard_map/all_to_all | solution.py:323
  50.0 0.9 %shard_map.138 = bf16[8,8,1280]{2,1,0:T(8,128)(2,1)} custom-call(bf16[16,8,5888]{2,1,0:T(8,128)(2,1)S(1)} %all_to_all.20.in_ref), custom_call_target="tpu_custom_call" | custom-call | tf_op jit(solution)/shard_map/pallas_call | solution.py:324
  50.9 8.6 %all-to-all-start.2 = ((bf16[8,8,1280]{2,1,0:T(8,128)(2,1)}), bf16[8,8,1280]{2,1,0:T(8,128)(2,1)S(1)}, u32[]{:S(2)}, u32[]{:S(2)}) async-start(bf16[8,8,1280]{2,1,0:T(8,128)(2,1)} %shard_map.138), calls=%async_computation.2 | async-start | bytes 327680 | tf_op jit(solution)/shard_map/all_to_all | solution.py:326
  59.5 0.6 collective-permute-start.2
  60.0 1.5 %collective-permute-start.3 = (bf16[32,768]{1,0:T(8,128)(2,1)S(1)}, bf16[32,768]{1,0:T(8,128)(2,1)S(1)}, u32[]{:S(2)}, u32[]{:S(2)}) collective-permute-start(bf16[32,768]{1,0:T(8,128)(2,1)S(1)} %get-tuple-element.40), channel_id=1, source_target_pairs={{0,4},{2,6},{4,0},{6,2},{1,5},{3,7},{5,1},{7,3},{8,12},{10,14},{12... | collective-permute-start | bytes 147464 | tf_op jit(solution)/shard_map/ppermute | solution.py:328
  61.5 1.8 %collective-permute-start.4 = (bf16[32,768]{1,0:T(8,128)(2,1)S(1)}, bf16[32,768]{1,0:T(8,128)(2,1)S(1)}, u32[]{:S(2)}, u32[]{:S(2)}) collective-permute-start(bf16[32,768]{1,0:T(8,128)(2,1)S(1)} %get-tuple-element.41), channel_id=1, source_target_pairs={{0,6},{2,0},{4,2},{6,4},{1,7},{3,1},{5,3},{7,5},{8,14},{10,8},{12,... | collective-permute-start | bytes 147464 | tf_op jit(solution)/shard_map/ppermute | solution.py:328
  63.3 1.5 %collective-permute-done.2.p1_ref = bf16[32,768]{1,0:T(8,128)(2,1)S(1)} collective-permute-done((bf16[32,768]{1,0:T(8,128)(2,1)S(1)}, bf16[32,768]{1,0:T(8,128)(2,1)S(1)}, u32[]{:S(2)}, u32[]{:S(2)}) %collective-permute-start.2) | collective-permute-done | bytes 49184 | tf_op jit(solution)/shard_map/ppermute | solution.py:328
  64.8 0.9 %collective-permute-done.3.p2_ref = bf16[32,768]{1,0:T(8,128)(2,1)S(1)} collective-permute-done((bf16[32,768]{1,0:T(8,128)(2,1)S(1)}, bf16[32,768]{1,0:T(8,128)(2,1)S(1)}, u32[]{:S(2)}, u32[]{:S(2)}) %collective-permute-start.3) | collective-permute-done | bytes 49184 | tf_op jit(solution)/shard_map/ppermute | solution.py:328
  65.6 0.5 collective-permute-done.4.p3_ref
  66.2 1.4 %shard_map.139 = bf16[128,1024]{1,0:T(8,128)(2,1)} custom-call(bf16[32,768]{1,0:T(8,128)(2,1)S(1)} %get-tuple-element.38.p0_ref, bf16[32,768]{1,0:T(8,128)(2,1)S(1)} %collective-permute-done.2.p1_ref, bf16[32,768]{1,0:T(8,128)(2,1)S(1)} %collective-permute-done.3.p2_ref, bf16[32,768]{1,0:T(8,128)(2,1)S(1)} %collective-permute-done.4.p3_ref, ...), custom_call_target="tpu_custom_call" | custom-call | tf_op jit(solution)/shard_map/pallas_call | solution.py:329
  67.5 0.0 all-to-all-done.2.in_ref
  67.5 0.7 shard_map.140
  68.2 4.7 %all-to-all-start.3 = ((bf16[16,8,512]{2,1,0:T(8,128)(2,1)}), bf16[16,8,512]{2,1,0:T(8,128)(2,1)S(1)}, u32[]{:S(2)}, u32[]{:S(2)}) async-start(bf16[16,8,512]{2,1,0:T(8,128)(2,1)} %get-tuple-element.46), calls=%async_computation.3 | async-start | bytes 262144 | tf_op jit(solution)/shard_map/all_to_all | solution.py:336
  72.9 0.6 reshape.32
  73.5 7.2 %all-to-all-done.3.in_ref = bf16[16,8,512]{2,1,0:T(8,128)(2,1)S(1)} async-done(((bf16[16,8,512]{2,1,0:T(8,128)(2,1)}), bf16[16,8,512]{2,1,0:T(8,128)(2,1)S(1)}, u32[]{:S(2)}, u32[]{:S(2)}) %all-to-all-start.3) | async-done | bytes 131104 | tf_op jit(solution)/shard_map/all_to_all | solution.py:336
  80.8 0.7 shard_map.141
Async XLA Ops:
  0.6 12.0 %all-to-all-start = ((bf16[8,16,1024]{2,1,0:T(8,128)(2,1)}), bf16[8,16,1024]{2,1,0:T(8,128)(2,1)S(1)}, u32[]{:S(2)}, u32[]{:S(2)}) async-start(bf16[8,16,1024]{2,1,0:T(8,128)(2,1)} %bitcast.11), calls=%async_computation | async-start | bytes 524288 | tf_op jit(solution)/shard_map/all_to_all | solution.py:298
  6.7 1.4 %copy-start = (bf16[1024,768]{1,0:T(8,128)(2,1)S(1)}, bf16[1024,768]{1,0:T(8,128)(2,1)}, u32[]{:S(2)}) copy-start(bf16[1024,768]{1,0:T(8,128)(2,1)} %proj_hbm.1) | copy-start | bytes 4718596
  8.1 4.6 %copy-start.1 = (bf16[32,768]{1,0:T(8,128)(2,1)S(1)}, bf16[32,768]{1,0:T(8,128)(2,1)}, u32[]{:S(2)}) copy-start(bf16[32,768]{1,0:T(8,128)(2,1)} %embed_ref.1) | copy-start | bytes 147460
  8.1 4.6 %copy-start.2 = (bf16[768,32]{0,1:T(8,128)(2,1)S(1)}, bf16[768,32]{0,1:T(8,128)(2,1)}, u32[]{:S(2)}) copy-start(bf16[768,32]{0,1:T(8,128)(2,1)} %param.13) | copy-start | bytes 147460
  20.0 2.3 %collective-permute-start.1 = (bf16[336,768]{1,0:T(8,128)(2,1)S(1)}, bf16[336,768]{1,0:T(8,128)(2,1)S(1)}, u32[]{:S(2)}, u32[]{:S(2)}) collective-permute-start(bf16[336,768]{1,0:T(8,128)(2,1)S(1)} %get-tuple-element.31.kg_ref), channel_id=1, source_target_pairs={{0,1},{1,0},{2,3},{3,2},{4,5},{5,4},{6,7},{7,6},{8,9},{9,8},{10,11... | collective-permute-start | bytes 1548296 | tf_op jit(solution)/shard_map/ppermute | solution.py:319
  20.1 2.2 %collective-permute-start = (bf16[128,896]{1,0:T(8,128)(2,1)S(1)}, bf16[128,896]{1,0:T(8,128)(2,1)S(1)}, u32[]{:S(2)}, u32[]{:S(2)}) collective-permute-start(bf16[128,896]{1,0:T(8,128)(2,1)S(1)} %get-tuple-element.30), channel_id=1, source_target_pairs={{0,1},{1,0},{2,3},{3,2},{4,5},{5,4},{6,7},{7,6},{8,9},{9,8},{10,11... | collective-permute-start | bytes 688136 | tf_op jit(solution)/shard_map/ppermute | solution.py:318
  50.9 16.6 %all-to-all-start.2 = ((bf16[8,8,1280]{2,1,0:T(8,128)(2,1)}), bf16[8,8,1280]{2,1,0:T(8,128)(2,1)S(1)}, u32[]{:S(2)}, u32[]{:S(2)}) async-start(bf16[8,8,1280]{2,1,0:T(8,128)(2,1)} %shard_map.138), calls=%async_computation.2 | async-start | bytes 327680 | tf_op jit(solution)/shard_map/all_to_all | solution.py:326
  59.5 5.3 %collective-permute-start.2 = (bf16[32,768]{1,0:T(8,128)(2,1)S(1)}, bf16[32,768]{1,0:T(8,128)(2,1)S(1)}, u32[]{:S(2)}, u32[]{:S(2)}) collective-permute-start(bf16[32,768]{1,0:T(8,128)(2,1)S(1)} %get-tuple-element.39), channel_id=1, source_target_pairs={{0,2},{2,4},{4,6},{6,0},{1,3},{3,5},{5,7},{7,1},{8,10},{10,12},{12... | collective-permute-start | bytes 147464 | tf_op jit(solution)/shard_map/ppermute | solution.py:328
  60.0 5.6 %collective-permute-start.3 = (bf16[32,768]{1,0:T(8,128)(2,1)S(1)}, bf16[32,768]{1,0:T(8,128)(2,1)S(1)}, u32[]{:S(2)}, u32[]{:S(2)}) collective-permute-start(bf16[32,768]{1,0:T(8,128)(2,1)S(1)} %get-tuple-element.40), channel_id=1, source_target_pairs={{0,4},{2,6},{4,0},{6,2},{1,5},{3,7},{5,1},{7,3},{8,12},{10,14},{12... | collective-permute-start | bytes 147464 | tf_op jit(solution)/shard_map/ppermute | solution.py:328
  61.5 4.7 %collective-permute-start.4 = (bf16[32,768]{1,0:T(8,128)(2,1)S(1)}, bf16[32,768]{1,0:T(8,128)(2,1)S(1)}, u32[]{:S(2)}, u32[]{:S(2)}) collective-permute-start(bf16[32,768]{1,0:T(8,128)(2,1)S(1)} %get-tuple-element.41), channel_id=1, source_target_pairs={{0,6},{2,0},{4,2},{6,4},{1,7},{3,1},{5,3},{7,5},{8,14},{10,8},{12,... | collective-permute-start | bytes 147464 | tf_op jit(solution)/shard_map/ppermute | solution.py:328
  68.2 12.6 %all-to-all-start.3 = ((bf16[16,8,512]{2,1,0:T(8,128)(2,1)}), bf16[16,8,512]{2,1,0:T(8,128)(2,1)S(1)}, u32[]{:S(2)}, u32[]{:S(2)}) async-start(bf16[16,8,512]{2,1,0:T(8,128)(2,1)} %get-tuple-element.46), calls=%async_computation.3 | async-start | bytes 262144 | tf_op jit(solution)/shard_map/all_to_all | solution.py:336

commit v5 on v4

--- a/solution.py
+++ b/solution.py
@@ -260,15 +260,21 @@
         out_ref[z, :, D:] = small
 
 
-def column_kernel(in_ref, proj_ref, attn_ref, small_ref):
-    total = in_ref[0].astype(F32)
+def small_kernel(in_ref, small_ref):
+    total = in_ref[0, :, D:].astype(F32)
     for s in range(1, NZ):
-        total = total + in_ref[s].astype(F32)
-    proj_ref[...] = total[0:4, :D]
-    attn_ref[...] = total[4:7, :D]
-    mine = total[:, D:].astype(BF16)
+        total = total + in_ref[s, :, D:].astype(F32)
+    mine = total.astype(BF16)
     for s in range(PLANE):
         small_ref[s] = mine
+
+
+def column_kernel(in_ref, proj_ref, attn_ref):
+    total = in_ref[0, :, :D].astype(F32)
+    for s in range(1, NZ):
+        total = total + in_ref[s, :, :D].astype(F32)
+    proj_ref[...] = total[0:4]
+    attn_ref[...] = total[4:7]
 
 
 def last_kernel(in_ref, head_ref, embed_ref, table_ref, loss_ref):
@@ -330,9 +336,8 @@
         back_kernel, [((ROWS, DGT), BF16)], scratch_shapes=[pltpu.VMEM((ROWS, D), BF16)]
     )(*back, proj_weight)
     columns, grad_global = lax.optimization_barrier((columns, grad_global))
-    grad_proj, grad_attn, small = call(
-        column_kernel, [((4, D), F32), ((3, D), F32), ((PLANE, 8, SMALL), BF16)]
-    )(columns)
+    (small,) = call(small_kernel, [((PLANE, 8, SMALL), BF16)])(columns)
+    grad_proj, grad_attn = call(column_kernel, [((4, D), F32), ((3, D), F32)])(columns)
     small = lax.all_to_all(small, plane, split_axis=0, concat_axis=0, tiled=True)
     head_rows, grad_embed, grad_table, loss = call(
         last_kernel,

time: 82 us -> 82 us (level)
  transfers between devices with their start and end apart: 8 -> 8, of which waited for: 6 -> 6; matrix products, arithmetic and copies ran while one was open for 3% -> 3% of each run, Pallas kernels for 2% -> 3%
where the time goes in v5:
time: 82 us; the launch traced here: 81.5 us
  blocking collectives  27.1 us (33%)
  starting transfers between devices  22.2 us (27%)
  waiting for transfers between devices  15.7 us (19%)
  Pallas kernels  12.2 us (15%)
  local copies, waits for them, and re-layouts  2.87 us (4%)
    all_to_all x1, blocking collectives, local(): lax.all_to_all(blocks, plane, split_axis=0, concat_axis=0, tiled=True)  27.1 us
    all_to_all x1, starting transfers between devices, local(): lax.all_to_all(columns, 'z', split_axis=0, concat_axis=0, tiled=True)  8.57 us
    pallas_call x1, Pallas kernels, local(): call(main_kernel, [((GROWS, D), BF16), (half, BF16), (half, BF16)], 50, i...  7.32 us
    all_to_all x1, waiting for transfers between devices, local(): lax.all_to_all(small, plane, split_axis=0, concat_axis=0, tiled=True)  6.61 us
    all_to_all x1, starting transfers between devices, local(): lax.all_to_all(small, plane, split_axis=0, concat_axis=0, tiled=True)  4.74 us
    all_to_all x1, starting transfers between devices, local(): lax.all_to_all(global_out.reshape(K, PD, DGT), ('y', 'c'), split_axis=0,...  4.48 us
    all_to_all x1, waiting for transfers between devices, local(): lax.all_to_all(global_out.reshape(K, PD, DGT), ('y', 'c'), split_axis=0,...  4.43 us
    ppermute x3, starting transfers between devices, local(): back[d] = lax.ppermute(back[d], 'y', [(s, (s + d) % NY) for s in range(NY)])  3.79 us
  transfers between devices with their start and end apart: 8, of which 6 were waited for; matrix products, arithmetic and copies ran while one was open for 3% of the time, Pallas kernels for 3%

profile of v5, /device:TPU:32, one launch (start us, length us, event | category | flops | bytes accessed | tf_op | source)
XLA Modules:
  0.0 81.5 jit_solution(17395503316327024003)
XLA Ops:
  0.6 4.5 %all-to-all-start = ((bf16[8,16,1024]{2,1,0:T(8,128)(2,1)}), bf16[8,16,1024]{2,1,0:T(8,128)(2,1)S(1)}, u32[]{:S(2)}, u32[]{:S(2)}) async-start(bf16[8,16,1024]{2,1,0:T(8,128)(2,1)} %bitcast.11), calls=%async_computation | async-start | bytes 524288 | tf_op jit(solution)/shard_map/all_to_all | solution.py:304
  5.1 0.8 copy.15
  5.9 0.7 add_bitcast_fusion
  6.6 0.1 reshape.31.nib_ref
  6.7 0.0 copy-start
  6.7 1.4 %copy-done = bf16[1024,768]{1,0:T(8,128)(2,1)S(1)} copy-done((bf16[1024,768]{1,0:T(8,128)(2,1)S(1)}, bf16[1024,768]{1,0:T(8,128)(2,1)}, u32[]{:S(2)}) %copy-start) | copy-done | bytes 1572888
  8.1 0.0 copy-start.1
  8.1 0.0 copy-start.2
  8.1 0.1 shard_map.135.proj_ref
  8.2 4.4 %all-to-all-done = bf16[8,16,1024]{2,1,0:T(8,128)(2,1)S(1)} async-done(((bf16[8,16,1024]{2,1,0:T(8,128)(2,1)}), bf16[8,16,1024]{2,1,0:T(8,128)(2,1)S(1)}, u32[]{:S(2)}, u32[]{:S(2)}) %all-to-all-start) | async-done | bytes 262176 | tf_op jit(solution)/shard_map/all_to_all | solution.py:304
  12.7 0.0 copy-done.1
  12.7 0.0 copy-done.2
  12.7 7.3 %shard_map.136 = (bf16[336,768]{1,0:T(8,128)(2,1)S(1)}, bf16[128,896]{1,0:T(8,128)(2,1)S(1)}, bf16[128,896]{1,0:T(8,128)(2,1)S(1)}) custom-call(bf16[128,1024]{1,0:T(8,128)(2,1)S(1)} %bitcast.8, s32[4,128]{1,0:T(4,128)S(1)} %reshape.31.nib_ref, bf16[1024,768]{1,0:T(8,128)(2,1)S(1)} %shard_map.135.proj_ref, bf16[32,768]{1,0:T(8,128)(2,1)S(1)} %copy-done.1, ...), custom_call_target="tpu_custom_call" | custom-call | tf_op jit(solution)/shard_map/pallas_call | solution.py:317
  20.0 0.1 collective-permute-start.1
  20.1 0.5 collective-permute-start
  20.6 1.7 %collective-permute-done.ra_ref = bf16[128,896]{1,0:T(8,128)(2,1)S(1)} collective-permute-done((bf16[128,896]{1,0:T(8,128)(2,1)S(1)}, bf16[128,896]{1,0:T(8,128)(2,1)S(1)}, u32[]{:S(2)}, u32[]{:S(2)}) %collective-permute-start) | collective-permute-done | bytes 229408 | tf_op jit(solution)/shard_map/ppermute | solution.py:324
  22.3 0.0 collective-permute-done.1.rg_ref
  22.3 0.6 shard_map.137
  22.9 27.1 %all_to_all.20.in_ref = bf16[16,8,5888]{2,1,0:T(8,128)(2,1)S(1)} all-to-all(bf16[16,8,5888]{2,1,0:T(8,128)(2,1)S(1)} %get-tuple-element.31), channel_id=1, replica_groups=mesh['x'=4,'z'=8,'y'=4,'c'=2] {'x','y'}, dimensions={0} | all-to-all | bytes 3014656 | tf_op jit(solution)/shard_map/all_to_all | solution.py:329
  50.0 0.9 %shard_map.138 = bf16[8,8,1280]{2,1,0:T(8,128)(2,1)} custom-call(bf16[16,8,5888]{2,1,0:T(8,128)(2,1)S(1)} %all_to_all.20.in_ref), custom_call_target="tpu_custom_call" | custom-call | tf_op jit(solution)/shard_map/pallas_call | solution.py:330
  50.9 8.6 %all-to-all-start.2 = ((bf16[8,8,1280]{2,1,0:T(8,128)(2,1)}), bf16[8,8,1280]{2,1,0:T(8,128)(2,1)S(1)}, u32[]{:S(2)}, u32[]{:S(2)}) async-start(bf16[8,8,1280]{2,1,0:T(8,128)(2,1)} %shard_map.138), calls=%async_computation.2 | async-start | bytes 327680 | tf_op jit(solution)/shard_map/all_to_all | solution.py:332
  59.5 0.6 collective-permute-start.2
  60.0 1.5 %collective-permute-start.3 = (bf16[32,768]{1,0:T(8,128)(2,1)S(1)}, bf16[32,768]{1,0:T(8,128)(2,1)S(1)}, u32[]{:S(2)}, u32[]{:S(2)}) collective-permute-start(bf16[32,768]{1,0:T(8,128)(2,1)S(1)} %get-tuple-element.39), channel_id=1, source_target_pairs={{0,4},{2,6},{4,0},{6,2},{1,5},{3,7},{5,1},{7,3},{8,12},{10,14},{12... | collective-permute-start | bytes 147464 | tf_op jit(solution)/shard_map/ppermute | solution.py:334
  61.5 1.8 %collective-permute-start.4 = (bf16[32,768]{1,0:T(8,128)(2,1)S(1)}, bf16[32,768]{1,0:T(8,128)(2,1)S(1)}, u32[]{:S(2)}, u32[]{:S(2)}) collective-permute-start(bf16[32,768]{1,0:T(8,128)(2,1)S(1)} %get-tuple-element.40), channel_id=1, source_target_pairs={{0,6},{2,0},{4,2},{6,4},{1,7},{3,1},{5,3},{7,5},{8,14},{10,8},{12,... | collective-permute-start | bytes 147464 | tf_op jit(solution)/shard_map/ppermute | solution.py:334
  63.3 1.5 %collective-permute-done.2.p1_ref = bf16[32,768]{1,0:T(8,128)(2,1)S(1)} collective-permute-done((bf16[32,768]{1,0:T(8,128)(2,1)S(1)}, bf16[32,768]{1,0:T(8,128)(2,1)S(1)}, u32[]{:S(2)}, u32[]{:S(2)}) %collective-permute-start.2) | collective-permute-done | bytes 49184 | tf_op jit(solution)/shard_map/ppermute | solution.py:334
  64.8 0.9 %collective-permute-done.3.p2_ref = bf16[32,768]{1,0:T(8,128)(2,1)S(1)} collective-permute-done((bf16[32,768]{1,0:T(8,128)(2,1)S(1)}, bf16[32,768]{1,0:T(8,128)(2,1)S(1)}, u32[]{:S(2)}, u32[]{:S(2)}) %collective-permute-start.3) | collective-permute-done | bytes 49184 | tf_op jit(solution)/shard_map/ppermute | solution.py:334
  65.6 0.5 collective-permute-done.4.p3_ref
  66.2 1.4 %shard_map.139 = bf16[128,1024]{1,0:T(8,128)(2,1)} custom-call(bf16[32,768]{1,0:T(8,128)(2,1)S(1)} %get-tuple-element.37.p0_ref, bf16[32,768]{1,0:T(8,128)(2,1)S(1)} %collective-permute-done.2.p1_ref, bf16[32,768]{1,0:T(8,128)(2,1)S(1)} %collective-permute-done.3.p2_ref, bf16[32,768]{1,0:T(8,128)(2,1)S(1)} %collective-permute-done.4.p3_ref, ...), custom_call_target="tpu_custom_call" | custom-call | tf_op jit(solution)/shard_map/pallas_call | solution.py:335
  67.5 0.0 all-to-all-done.2.in_ref
  67.5 0.7 shard_map.141
  68.2 4.7 %all-to-all-start.3 = ((bf16[16,8,512]{2,1,0:T(8,128)(2,1)}), bf16[16,8,512]{2,1,0:T(8,128)(2,1)S(1)}, u32[]{:S(2)}, u32[]{:S(2)}) async-start(bf16[16,8,512]{2,1,0:T(8,128)(2,1)} %shard_map.141), calls=%async_computation.3 | async-start | bytes 262144 | tf_op jit(solution)/shard_map/all_to_all | solution.py:341
  72.9 0.6 shard_map.140
  73.5 0.6 reshape.32
  74.2 6.6 %all-to-all-done.3.in_ref = bf16[16,8,512]{2,1,0:T(8,128)(2,1)S(1)} async-done(((bf16[16,8,512]{2,1,0:T(8,128)(2,1)}), bf16[16,8,512]{2,1,0:T(8,128)(2,1)S(1)}, u32[]{:S(2)}, u32[]{:S(2)}) %all-to-all-start.3) | async-done | bytes 131104 | tf_op jit(solution)/shard_map/all_to_all | solution.py:341
  80.8 0.7 shard_map.142
Async XLA Ops:
  0.6 12.0 %all-to-all-start = ((bf16[8,16,1024]{2,1,0:T(8,128)(2,1)}), bf16[8,16,1024]{2,1,0:T(8,128)(2,1)S(1)}, u32[]{:S(2)}, u32[]{:S(2)}) async-start(bf16[8,16,1024]{2,1,0:T(8,128)(2,1)} %bitcast.11), calls=%async_computation | async-start | bytes 524288 | tf_op jit(solution)/shard_map/all_to_all | solution.py:304
  6.7 1.4 %copy-start = (bf16[1024,768]{1,0:T(8,128)(2,1)S(1)}, bf16[1024,768]{1,0:T(8,128)(2,1)}, u32[]{:S(2)}) copy-start(bf16[1024,768]{1,0:T(8,128)(2,1)} %proj_hbm.1) | copy-start | bytes 4718596
  8.1 4.6 %copy-start.1 = (bf16[32,768]{1,0:T(8,128)(2,1)S(1)}, bf16[32,768]{1,0:T(8,128)(2,1)}, u32[]{:S(2)}) copy-start(bf16[32,768]{1,0:T(8,128)(2,1)} %embed_ref.1) | copy-start | bytes 147460
  8.1 4.6 %copy-start.2 = (bf16[768,32]{0,1:T(8,128)(2,1)S(1)}, bf16[768,32]{0,1:T(8,128)(2,1)}, u32[]{:S(2)}) copy-start(bf16[768,32]{0,1:T(8,128)(2,1)} %param.13) | copy-start | bytes 147460
  20.0 2.3 %collective-permute-start.1 = (bf16[336,768]{1,0:T(8,128)(2,1)S(1)}, bf16[336,768]{1,0:T(8,128)(2,1)S(1)}, u32[]{:S(2)}, u32[]{:S(2)}) collective-permute-start(bf16[336,768]{1,0:T(8,128)(2,1)S(1)} %get-tuple-element.30.kg_ref), channel_id=1, source_target_pairs={{0,1},{1,0},{2,3},{3,2},{4,5},{5,4},{6,7},{7,6},{8,9},{9,8},{10,11... | collective-permute-start | bytes 1548296 | tf_op jit(solution)/shard_map/ppermute | solution.py:325
  20.1 2.2 %collective-permute-start = (bf16[128,896]{1,0:T(8,128)(2,1)S(1)}, bf16[128,896]{1,0:T(8,128)(2,1)S(1)}, u32[]{:S(2)}, u32[]{:S(2)}) collective-permute-start(bf16[128,896]{1,0:T(8,128)(2,1)S(1)} %get-tuple-element.29), channel_id=1, source_target_pairs={{0,1},{1,0},{2,3},{3,2},{4,5},{5,4},{6,7},{7,6},{8,9},{9,8},{10,11... | collective-permute-start | bytes 688136 | tf_op jit(solution)/shard_map/ppermute | solution.py:324
  50.9 16.6 %all-to-all-start.2 = ((bf16[8,8,1280]{2,1,0:T(8,128)(2,1)}), bf16[8,8,1280]{2,1,0:T(8,128)(2,1)S(1)}, u32[]{:S(2)}, u32[]{:S(2)}) async-start(bf16[8,8,1280]{2,1,0:T(8,128)(2,1)} %shard_map.138), calls=%async_computation.2 | async-start | bytes 327680 | tf_op jit(solution)/shard_map/all_to_all | solution.py:332
  59.5 5.3 %collective-permute-start.2 = (bf16[32,768]{1,0:T(8,128)(2,1)S(1)}, bf16[32,768]{1,0:T(8,128)(2,1)S(1)}, u32[]{:S(2)}, u32[]{:S(2)}) collective-permute-start(bf16[32,768]{1,0:T(8,128)(2,1)S(1)} %get-tuple-element.38), channel_id=1, source_target_pairs={{0,2},{2,4},{4,6},{6,0},{1,3},{3,5},{5,7},{7,1},{8,10},{10,12},{12... | collective-permute-start | bytes 147464 | tf_op jit(solution)/shard_map/ppermute | solution.py:334
  60.0 5.6 %collective-permute-start.3 = (bf16[32,768]{1,0:T(8,128)(2,1)S(1)}, bf16[32,768]{1,0:T(8,128)(2,1)S(1)}, u32[]{:S(2)}, u32[]{:S(2)}) collective-permute-start(bf16[32,768]{1,0:T(8,128)(2,1)S(1)} %get-tuple-element.39), channel_id=1, source_target_pairs={{0,4},{2,6},{4,0},{6,2},{1,5},{3,7},{5,1},{7,3},{8,12},{10,14},{12... | collective-permute-start | bytes 147464 | tf_op jit(solution)/shard_map/ppermute | solution.py:334
  61.5 4.7 %collective-permute-start.4 = (bf16[32,768]{1,0:T(8,128)(2,1)S(1)}, bf16[32,768]{1,0:T(8,128)(2,1)S(1)}, u32[]{:S(2)}, u32[]{:S(2)}) collective-permute-start(bf16[32,768]{1,0:T(8,128)(2,1)S(1)} %get-tuple-element.40), channel_id=1, source_target_pairs={{0,6},{2,0},{4,2},{6,4},{1,7},{3,1},{5,3},{7,5},{8,14},{10,8},{12,... | collective-permute-start | bytes 147464 | tf_op jit(solution)/shard_map/ppermute | solution.py:334
  68.2 12.6 %all-to-all-start.3 = ((bf16[16,8,512]{2,1,0:T(8,128)(2,1)}), bf16[16,8,512]{2,1,0:T(8,128)(2,1)S(1)}, u32[]{:S(2)}, u32[]{:S(2)}) async-start(bf16[16,8,512]{2,1,0:T(8,128)(2,1)} %shard_map.141), calls=%async_computation.3 | async-start | bytes 262144 | tf_op jit(solution)/shard_map/all_to_all | solution.py:341
